TPU v7x, 32 devices: a whole 2x2x4 slice. The times are simulated.
32 devices in a mesh: src: 8 (over z, core), tgt: 4 (over y, x).
Axes of the slice: x: 2, y: 2, z: 4, core: 2. Of those that a mesh axis runs over, the one named last changes fastest.
Arguments:
- src_pts: float32 [64, 8192], P('tgt', 'src'), may hold values from -30 to 30
- tgt_pts: float32 [64, 8192], P('src', 'tgt'), may hold values from -6 to 6
- src_mass: float32 [8192], P('src'), may hold values from 0.1 to 1
- tgt_mass: float32 [8192], P('tgt'), may hold values from 0.1 to 1
- init_pot: float32 [8192], P('tgt'), may hold values from -3 to 3
Outputs:
- src_pot: float32 [8192], P('src')
- tgt_pot: float32 [8192], P('tgt')
- mapped: float32 [64, 8192], P('tgt', 'src')
All inputs are finite; a program needn't handle non-finite values.
Results may differ from a plain program's by a relative error of at most 0.0003.
Values sent between devices are 32-bit elements; how exact they have to be, the bound alone decides.
No kernel may reach another device: no remote copies, remote signals or barrier semaphores. Data moves between devices by JAX's collectives and lax.ppermute only.
A program may use at most 64 MiB of HBM per device.

v0:
```python
import functools
import math

import jax
import jax.numpy as jnp
from jax import lax
from jax.experimental import pallas as pl
from jax.experimental.pallas import tpu as pltpu
from jax.sharding import PartitionSpec as P

ITERS = 3
EPS = 0.1
UNIT = EPS * math.log(2.0)
LOW = 2.0**-40
HIGH = 2.0**20

F32 = jnp.float32
BF16 = jnp.bfloat16
VMEM = pl.BlockSpec(memory_space=pltpu.VMEM)
SMEM = pl.BlockSpec(memory_space=pltpu.SMEM)
HBM = pl.BlockSpec(memory_space=pltpu.HBM)
LANES = 128


def pieces(v):
    a = v.astype(BF16)
    r = v - a.astype(F32)
    b = r.astype(BF16)
    c = (r - b.astype(F32)).astype(BF16)
    return a, b, c


def tree(op, items):
    items = list(items)
    while len(items) > 1:
        half = (len(items) + 1) // 2
        rest = items[half:]
        items = [op(items[k], rest[k]) if k < len(rest) else items[k] for k in range(half)]
    return items[0]


def whole_log_sum(part_refs):
    if len(part_refs) == 1:
        parts = [part_refs[0][t] for t in range(part_refs[0].shape[0])]
    else:
        parts = [p[0] for p in part_refs]
    top = tree(jnp.maximum, parts)
    return top + jnp.log2(tree(jnp.add, [jnp.exp2(p - top) for p in parts]))


def to_row(wide):
    split = jnp.concatenate(pieces(wide), axis=1)
    ones = jnp.ones((16, split.shape[1]), BF16)
    return lax.dot_general(ones, split, (((1,), (1,)), ((), ())), preferred_element_type=F32)[0:1, :]


def across(row, out_ref):
    n = row.shape[1]
    a, b, c = [p.astype(F32) for p in pieces(row)]
    at = lax.broadcasted_iota(jnp.int32, (16, n), 0)
    split = jnp.where(at == 0, a, jnp.where(at == 1, b, jnp.where(at == 2, c, 0.0))).astype(BF16)
    ones = jnp.ones((16, LANES), BF16)
    out_ref[...] = lax.dot_general(split, ones, (((0,), (0,)), ((), ())), preferred_element_type=F32)


def eight(k):
    return pl.ds(pl.multiple_of(k * 8, 8), 8)


def chunk(c):
    return pl.ds(c * LANES, LANES)


def lanes_log_sum(s_ref, rows, pot8, top_ref, sum_ref):
    cols = s_ref.shape[1] // LANES
    z = [s_ref[rows, chunk(c)] + pot8[:, c * LANES : (c + 1) * LANES] for c in range(cols)]
    top = tree(jnp.maximum, z)
    top_ref[rows, :] = top
    sum_ref[rows, :] = tree(jnp.add, [jnp.exp2(v - top) for v in z])


def join_lanes(top_ref, sum_ref):
    def strip(k, _):
        rows = eight(k)
        part = top_ref[rows, :]
        top = jnp.broadcast_to(jnp.max(part, axis=1, keepdims=True), part.shape)
        sum_ref[rows, :] = sum_ref[rows, :] * jnp.exp2(part - top)
        top_ref[rows, :] = top * (1.0 / LANES)
        return 0

    lax.fori_loop(0, top_ref.shape[0] // 8, strip, 0, unroll=16)
    return to_row(top_ref[...]) + jnp.log2(to_row(sum_ref[...]))


def rows_log_sum(s_ref, pot, top_ref, sum_ref):
    n, width = s_ref.shape
    pot8 = jnp.broadcast_to(pot, (8, width))

    def strip(k, _):
        lanes_log_sum(s_ref, eight(k), pot8, top_ref, sum_ref)
        return 0

    lax.fori_loop(0, n // 8, strip, 0, unroll=4)
    return join_lanes(top_ref, sum_ref)


def cols_log_sum(s_ref, pot_ref):
    n, width = s_ref.shape
    cols = width // LANES

    def load(k):
        rows = eight(k)
        f = pot_ref[rows, :]
        return [s_ref[rows, chunk(c)] + f for c in range(cols)]

    def find(k, top):
        return tuple(jnp.maximum(t, v) for t, v in zip(top, load(k)))

    top = lax.fori_loop(1, n // 8, find, tuple(load(0)), unroll=4)

    def add(k, total):
        return tuple(a + jnp.exp2(v - t) for a, v, t in zip(total, load(k), top))

    zero = tuple(jnp.zeros((8, LANES), F32) for _ in range(cols))
    total = lax.fori_loop(0, n // 8, add, zero, unroll=4)
    out = []
    for t, a in zip(top, total):
        m = jnp.max(t, axis=0, keepdims=True)
        out.append(m + jnp.log2(jnp.sum(a * jnp.exp2(t - m), axis=0, keepdims=True)))
    return jnp.concatenate(out, axis=1)


def repeat(row, out_ref):
    for t in range(out_ref.shape[0]):
        out_ref[t] = row


def sum_kernel(*refs):
    refs[-1][0] = whole_log_sum(refs[:-1])


def early_kernel(mass_ref, pot_ref, x_ref, ls_ref, to_ref, xo_ref):
    ls_ref[...] = jnp.log2(mass_ref[...])
    to_ref[...] = pot_ref[...]
    xo_ref[...] = x_ref[...]


def first_kernel(peers, xplan, yplan, me_ref, pot_ref, *refs):
    xcount, ycount = len(xplan), len(yplan)
    xparts, yparts, refs = refs[:xcount], refs[xcount : xcount + ycount], refs[xcount + ycount :]
    s_ref, l_ref, xn_ref, yn_ref, yo_ref, xs, xw, yw, top_ref, sum_ref = refs
    me_src, me_tgt = me_ref[0] // peers, lax.rem(me_ref[0], peers)
    for part, d in zip(xparts, xplan):
        if d is None:
            xs[...] = part[...]
            continue
        own = part.shape[0]
        xs[pl.ds(pl.multiple_of(lax.rem(me_tgt - d + peers, peers) * own, 8), own), :] = part[...]
    x = xs[...]
    xn_ref[...] = jnp.sum(x * x, axis=0, keepdims=True) / x.shape[0]
    x1, x2, x3 = pieces(x)
    for part, owners in zip(yparts, yplan):
        if owners is None:
            yo_ref[...] = part[...]
            continue
        own = part.shape[0] // len(owners)
        for b, d in enumerate(owners):
            yo_ref[pl.ds(pl.multiple_of((me_src ^ d) * own, 8), own), :] = part[pl.ds(b * own, own), :]
    y = yo_ref[...]
    yn = jnp.sum(y * y, axis=0, keepdims=True) / y.shape[0]
    yn_ref[...] = yn
    k = y.shape[0]
    y1, y2, y3 = pieces(y * (2.0 / (k * UNIT)))
    for p, (xp, yp) in enumerate(((x1, y1), (x1, y2), (x2, y1), (x2, y2), (x1, y3), (x3, y1))):
        xw[pl.ds(p * k, k), :] = xp
        yw[pl.ds(p * k, k), :] = yp
    n, width = s_ref.shape
    pot8 = jnp.broadcast_to((pot_ref[...] - yn) * (1.0 / UNIT), (8, width))
    step = 256
    for b in range(n // step + 1):
        if b < n // step:
            s_ref[pl.ds(b * step, step), :] = lax.dot_general(
                xw[:, pl.ds(b * step, step)], yw[...], (((0,), (0,)), ((), ())), preferred_element_type=F32
            )
        if b > 0:
            for r in range((b - 1) * step, b * step, 8):
                lanes_log_sum(s_ref, pl.ds(r, 8), pot8, top_ref, sum_ref)
    l_ref[0] = join_lanes(top_ref, sum_ref)


def src_first_kernel(count, s_ref, mass_ref, *refs):
    parts, (f_ref, wide_ref, l_ref) = refs[:count], refs[count:]
    f = mass_ref[...] - whole_log_sum(parts)
    f_ref[...] = f
    across(f, wide_ref)
    repeat(cols_log_sum(s_ref, wide_ref), l_ref)


def tgt_first_kernel(count, s_ref, mass_ref, f_ref, wide_ref, *refs):
    parts, (g_ref, p_ref, l_ref, top_ref, sum_ref) = refs[:count], refs[count:]
    n, width = s_ref.shape
    g = jnp.log2(mass_ref[...]) - whole_log_sum(parts)
    g_ref[...] = g
    g8 = jnp.broadcast_to(g, (8, width))

    def strip(k, _):
        rows = eight(k)
        f = wide_ref[rows, :]
        out = []
        for c in range(width // LANES):
            p = jnp.exp2((s_ref[rows, chunk(c)] + f) + g8[:, c * LANES : (c + 1) * LANES])
            p_ref[rows, chunk(c)] = p
            out.append(p)
        sum_ref[rows, :] = tree(jnp.add, out)
        return 0

    lax.fori_loop(0, n // 8, strip, 0, unroll=4)
    total = to_row(sum_ref[...])
    l_ref[0] = jnp.log2(total)

    @pl.when(jnp.logical_not(jnp.min(total) >= LOW))
    def _():
        l_ref[0] = f_ref[...] + rows_log_sum(s_ref, g, top_ref, sum_ref)


def src_kernel(count, s_ref, p_ref, mass_ref, f_ref, g_ref, *refs):
    parts, (*u_refs, l_ref, wide) = refs[:count], refs[count:]
    n, width = p_ref.shape
    cols = width // LANES
    change = mass_ref[...] - whole_log_sum(parts)
    for u_ref in u_refs:
        u_ref[...] = change
    u = jnp.exp2(change)
    across(u, wide)

    def add(k, total):
        rows = eight(k)
        f = wide[rows, :]
        return tuple(a + p_ref[rows, chunk(c)] * f for c, a in enumerate(total))

    zero = tuple(jnp.zeros((8, LANES), F32) for _ in range(cols))
    parts = lax.fori_loop(0, n // 8, add, zero, unroll=4)
    total = jnp.concatenate([jnp.sum(a, axis=0, keepdims=True) for a in parts], axis=1)
    repeat(jnp.log2(total), l_ref)
    fine = jnp.logical_and(jnp.min(total) >= LOW, jnp.max(u) <= HIGH)

    @pl.when(jnp.logical_not(fine))
    def _():
        across(f_ref[...] + change, wide)
        repeat(g_ref[...] + cols_log_sum(s_ref, wide), l_ref)


def tgt_kernel(count, s_ref, p_ref, mass_ref, f_ref, g_ref, *refs):
    parts, (l_ref, top_ref, sum_ref) = refs[:count], refs[count:]
    n, width = p_ref.shape
    change = jnp.log2(mass_ref[...]) - whole_log_sum(parts)
    v = jnp.exp2(change)
    v8 = jnp.broadcast_to(v, (8, width))

    def strip(k, _):
        rows = eight(k)
        sum_ref[rows, :] = tree(
            jnp.add, [p_ref[rows, chunk(c)] * v8[:, c * LANES : (c + 1) * LANES] for c in range(width // LANES)]
        )
        return 0

    lax.fori_loop(0, n // 8, strip, 0, unroll=4)
    total = to_row(sum_ref[...])
    l_ref[0] = jnp.log2(total)
    fine = jnp.logical_and(jnp.min(total) >= LOW, jnp.max(v) <= HIGH)

    @pl.when(jnp.logical_not(fine))
    def _():
        l_ref[0] = f_ref[...] + rows_log_sum(s_ref, g_ref[...] + change, top_ref, sum_ref)


def last_kernel(count, me_ref, s_ref, p_ref, mass_ref, f_ref, g_ref, u_ref, xn_ref, yn_ref, y_ref, *refs):
    parts, refs = refs[:count], refs[count:]
    sp_any, tp_any, outs = refs[0], refs[1], refs[2:-7]
    sp, tp, yw, acc, flat, wide, sem = refs[-7:]
    k = y_ref.shape[0]
    n, width = s_ref.shape
    peers = len(outs)
    own = k // peers
    block = own + 1
    change = jnp.log2(mass_ref[...]) - whole_log_sum(parts)
    g = g_ref[...] + change
    f = f_ref[...] + u_ref[...]
    sp[...] = f * UNIT + xn_ref[...]
    tp[...] = g * UNIT + yn_ref[...]
    copies = [pltpu.make_async_copy(sp, sp_any, sem.at[0]), pltpu.make_async_copy(tp, tp_any, sem.at[1])]
    for copy in copies:
        copy.start()
    u = jnp.exp2(u_ref[...])
    v = jnp.exp2(change)
    step = 256

    def project(weight, scale, rescale):
        y1, y2, _ = pieces(y_ref[...] * scale)
        s1, s2, _ = [p.astype(F32) for p in pieces(scale)]
        yw[pl.ds(0, k), :] = y1
        at = lax.broadcasted_iota(jnp.int32, (LANES - k, width), 0)
        yw[pl.ds(k, LANES - k), :] = jnp.where(at == 0, s1, jnp.where(at == 1, s2, 0.0)).astype(BF16)
        yw[pl.ds(LANES, k), :] = y2
        yw[pl.ds(LANES + k, LANES - k), :] = jnp.zeros((LANES - k, width), BF16)
        for b in range(n // step):
            w = weight(pl.ds(b * step, step))
            w1 = w.astype(BF16)
            w2 = (w - w1.astype(F32)).astype(BF16)
            dims = (((1,), (1,)), ((), ()))
            out = lax.dot_general(w1, yw[...], dims, preferred_element_type=F32) + lax.dot_general(
                w2, yw[...], dims, preferred_element_type=F32
            )
            acc[pl.ds(b * step, step), :] = out[:, :LANES] + out[:, LANES:]
        total = acc[...].T * rescale
        den = total[k : k + 1, :] + total[k + 1 : k + 2, :]
        for t in range(peers):
            for c in range(n // LANES):
                at = slice(c * LANES, (c + 1) * LANES)
                flat[t, pl.ds(c * block, own), :] = total[t * own : (t + 1) * own, at]
                flat[t, pl.ds(c * block + own, 1), :] = den[:, at]
        for d, out in enumerate(outs):
            out[...] = flat[lax.rem(me_ref[0] + d, peers)]
        return den

    den = project(lambda rows: p_ref[rows, :], v, u)
    fine = jnp.logical_and(jnp.min(den) >= LOW, jnp.logical_and(jnp.max(u) <= HIGH, jnp.max(v) <= HIGH))

    @pl.when(jnp.logical_not(fine))
    def _():
        across(f, wide)

        def weight(rows):
            fb = jnp.concatenate([wide[rows, :]] * (width // LANES), axis=1)
            return jnp.exp2((s_ref[rows, :] + fb) + g)

        project(weight, jnp.ones_like(v), jnp.ones_like(u))

    for copy in copies:
        copy.wait()


def join_kernel(*refs):
    parts, out_ref = refs[:-1], refs[-1]
    own, n = out_ref.shape
    for c in range(n // LANES):
        at = c * (own + 1)
        num = tree(jnp.add, [p[pl.ds(at, own), :] for p in parts])
        den = tree(jnp.add, [p[pl.ds(at + own, 1), :] for p in parts])
        out_ref[:, chunk(c)] = num / den


def call(kernel, outs, scratch, ins, out_specs=None):
    return pl.pallas_call(
        kernel,
        out_shape=[o if isinstance(o, jax.ShapeDtypeStruct) else jax.ShapeDtypeStruct(o, F32) for o in outs],
        in_specs=[spec for spec, _ in ins],
        out_specs=out_specs or [VMEM] * len(outs),
        scratch_shapes=scratch,
        compiler_params=pltpu.CompilerParams(vmem_limit_bytes=20 * 2**20),
    )(*[a for _, a in ins])


def put(*arrays):
    return [(VMEM, a) for a in arrays]


def turn(v, axis, size, d):
    return lax.ppermute(v, axis, [(i, (i + d) % size) for i in range(size)])


def flip(v, axis, size, bit):
    return lax.ppermute(v, axis, [(i, i ^ bit) for i in range(size)])


def join_rows(v, axis, size):
    if spread(size) > 1:
        return [lax.all_to_all(v, axis, 0, 0, tiled=True)]
    parts, bit = [v], 1
    while bit < size:
        if bit > 1:
            parts = call(sum_kernel, [v.shape], [], put(*parts))
        parts = [parts[0], flip(parts[0], axis, size, bit)]
        bit *= 2
    return parts


def spread(size):
    return 1 if size in (2, 4, 8) else size


def gather_src(v, size):
    if v.shape[0] % 8 or size > 4:
        return [lax.all_gather(v, "tgt", axis=0, tiled=True)], [None]
    return [v] + [turn(v, "tgt", size, d) for d in range(1, size)], list(range(size))


def gather_tgt(v, size, other):
    if v.shape[0] % 8 or size & (size - 1):
        return [lax.all_gather(v, "src", axis=0, tiled=True)], [None], other
    order = list(range(0, size, 2))
    mine = jnp.concatenate([v] + [flip(v, "src", size, d) for d in order[1:]], axis=0)
    mine, *early = lax.optimization_barrier([mine] + other[:-1])
    other = early + other[-1:]
    return [mine, flip(mine, "src", size, 1)], [order, [d + 1 for d in order]], other


def shards(peers_src, peers_tgt, src_pts, tgt_pts, src_mass, tgt_mass, init_pot):
    own = src_pts.shape[0]
    n, width = src_pts.shape[1], tgt_pts.shape[1]
    k = own * peers_tgt
    pack = (own + 1) * (n // LANES)
    row, col = (1, n), (1, width)
    rows, cols = (spread(peers_tgt), 1, n), (spread(peers_src), 1, width)
    lane = pltpu.VMEM((n, LANES), F32)
    me = lax.axis_index(("src", "tgt")).astype(jnp.int32).reshape(1)
    xs, xplan = gather_src(src_pts, peers_tgt)
    sm, pot = src_mass.reshape(row), init_pot.reshape(col)
    ys, yplan, (sm, pot, *xs) = gather_tgt(tgt_pts, peers_src, [sm, pot] + xs)
    tm = tgt_mass.reshape(col)
    sm, pot, x = call(early_kernel, [row, col, xs[0].shape], [], put(sm, pot, xs[0]))
    s, l, xn, yn, yo = call(
        functools.partial(first_kernel, peers_tgt, xplan, yplan),
        [(n, width), rows, row, col, (k, width)],
        [pltpu.VMEM((k, n), F32), pltpu.VMEM((6 * k, n), BF16), pltpu.VMEM((6 * k, width), BF16), lane, lane],
        [(SMEM, me)] + put(pot, x, *xs[1:], *ys),
    )
    parts = join_rows(l, "tgt", peers_tgt)
    f, wide, l = call(
        functools.partial(src_first_kernel, len(parts)), [row, (n, LANES), cols], [], put(s, sm, *parts)
    )
    parts = join_rows(l, "src", peers_src)
    g, p, l = call(
        functools.partial(tgt_first_kernel, len(parts)),
        [col, (n, width), rows],
        [lane, lane],
        put(s, tm, f, wide, *parts),
    )
    for step in range(1, ITERS):
        parts = join_rows(l, "tgt", peers_tgt)
        *u, l = call(
            functools.partial(src_kernel, len(parts)),
            [row, cols] if step == ITERS - 1 else [cols],
            [lane],
            put(s, p, sm, f, g, *parts),
        )
        parts = join_rows(l, "src", peers_src)
        if step < ITERS - 1:
            (l,) = call(functools.partial(tgt_kernel, len(parts)), [rows], [lane, lane], put(s, p, tm, f, g, *parts))
    src_pot, tgt_pot, *blocks = call(
        functools.partial(last_kernel, len(parts)),
        [row, col] + [(pack, LANES)] * peers_tgt,
        [
            pltpu.VMEM(row, F32),
            pltpu.VMEM(col, F32),
            pltpu.VMEM((2 * LANES, width), BF16),
            lane,
            pltpu.VMEM((peers_tgt, pack, LANES), F32),
            lane,
            pltpu.SemaphoreType.DMA((2,)),
        ],
        [(SMEM, me)] + put(s, p, tm, f, g, *u, xn, yn, yo, *parts),
        [HBM, HBM] + [VMEM] * peers_tgt,
    )
    came = [blocks[0]] + [turn(blocks[d], "tgt", peers_tgt, d) for d in range(1, peers_tgt)]
    (mapped,) = call(join_kernel, [(own, n)], [], put(*came))
    return src_pot.reshape(n), tgt_pot.reshape(width), mapped


def solution(mesh):
    return jax.shard_map(
        functools.partial(shards, mesh.shape["src"], mesh.shape["tgt"]),
        mesh=mesh,
        in_specs=(P("tgt", "src"), P("src", "tgt"), P("src"), P("tgt"), P("tgt")),
        out_specs=(P("src"), P("tgt"), P("tgt", "src")),
        check_vma=False,
    )
```

profile of v0, /device:TPU:0, one launch (start us, length us, event | category | flops | bytes accessed | tf_op | source)
XLA Modules:
  0.0 102.8 jit_solution(1838259920022823994)
XLA Ops:
  0.6 4.1 %collective-permute-start.1 = (f32[8,2048]{1,0:T(8,128)}, f32[8,2048]{1,0:T(8,128)S(1)}, u32[]{:S(2)}, u32[]{:S(2)}) collective-permute-start(f32[8,2048]{1,0:T(8,128)} %param.6), channel_id=1, source_target_pairs={{0,16},{4,20},{8,24},{12,28},{16,0},{20,4},{24,8},{28,12},{1,17},{... | collective-permute-start | bytes 196616 | tf_op jit(solution)/shard_map/ppermute | solution.py:373
  9.6 3.0 %collective-permute-done.2 = f32[8,2048]{1,0:T(8,128)S(1)} collective-permute-done((f32[8,2048]{1,0:T(8,128)}, f32[8,2048]{1,0:T(8,128)S(1)}, u32[]{:S(2)}, u32[]{:S(2)}) %collective-permute-start.2) | collective-permute-done | bytes 65568 | tf_op jit(solution)/shard_map/ppermute | solution.py:373
  13.6 2.5 %collective-permute-start.5 = (f32[16,1024]{1,0:T(8,128)}, f32[16,1024]{1,0:T(8,128)S(1)}, u32[]{:S(2)}, u32[]{:S(2)}) collective-permute-start(f32[16,1024]{1,0:T(8,128)} %x_ref), channel_id=1, source_target_pairs={{0,3},{1,0},{2,1},{3,2},{4,7},{5,4},{6,5},{7,6},{8,11},{9,8},{10,9... | collective-permute-start | bytes 196616 | tf_op jit(solution)/shard_map/ppermute | solution.py:369
  18.3 4.5 %shard_map.77 = (f32[1024,2048]{1,0:T(8,128)S(1)}, f32[1,1,1024]{2,1,0:T(1,128)S(1)}, f32[1,1024]{1,0:T(1,128)S(1)}, f32[1,2048]{1,0:T(1,128)S(1)}, f32[64,2048]{1,0:T(8,128)S(1)}) custom-call(s32[1]{0:T(128)} %bitcast.me_ref, f32[1,2048]{1,0:T(1,128)S(1)} %get-tuple-element.34.pot_ref, f32[16,1024]{1,0:T(8,128)S(1)} %get-tuple-element.35.refs_0_, ...), custom_call_target="tpu_custom_call" | custom-call | tf_op jit(solution)/shard_map/pallas_call | solution.py:354
  22.9 2.3 %collective-permute-start.7 = (f32[1,1,1024]{2,1,0:T(1,128)S(1)}, f32[1,1,1024]{2,1,0:T(1,128)S(1)}, u32[]{:S(2)}, u32[]{:S(2)}) collective-permute-start(f32[1,1,1024]{2,1,0:T(1,128)S(1)} %get-tuple-element.41.refs_0_), channel_id=1, source_target_pairs={{0,1},{1,0},{2,3},{3,2},{4,5},{5,4},{6,7},{7,6},{8,9},{9,8},{10,11... | collective-permute-start | bytes 12296 | tf_op jit(solution)/shard_map/ppermute | solution.py:373
  28.4 2.1 %collective-permute-done.8.refs_1_ = f32[1,1,1024]{2,1,0:T(1,128)S(1)} collective-permute-done((f32[1,1,1024]{2,1,0:T(1,128)S(1)}, f32[1,1,1024]{2,1,0:T(1,128)S(1)}, u32[]{:S(2)}, u32[]{:S(2)}) %collective-permute-start.8) | collective-permute-done | bytes 4128 | tf_op jit(solution)/shard_map/ppermute | solution.py:373
  30.5 2.7 %shard_map.79 = (f32[1,1024]{1,0:T(1,128)S(1)}, f32[1024,128]{1,0:T(8,128)S(1)}, f32[1,1,2048]{2,1,0:T(1,128)S(1)}) custom-call(f32[1024,2048]{1,0:T(8,128)S(1)} %get-tuple-element.39.s_ref, f32[1,1024]{1,0:T(1,128)S(1)} %get-tuple-element.40.mass_ref, f32[1,1,1024]{2,1,0:T(1,128)S(1)} %shard_map.78.refs_0_, f32[1,1,1024]{2,1,0:T(1,128)S(1)} %collective-permute-done.8.refs_1_), custom_call_target="tpu_custom_call" | custom-call | tf_op jit(solution)/shard_map/pallas_call | solution.py:354
  34.7 3.4 %collective-permute-done.10.refs_1_ = f32[1,1,2048]{2,1,0:T(1,128)S(1)} collective-permute-done((f32[1,1,2048]{2,1,0:T(1,128)S(1)}, f32[1,1,2048]{2,1,0:T(1,128)S(1)}, u32[]{:S(2)}, u32[]{:S(2)}) %collective-permute-start.10) | collective-permute-done | bytes 8224 | tf_op jit(solution)/shard_map/ppermute | solution.py:373
  39.9 2.9 %collective-permute-done.11.refs_1_ = f32[1,1,2048]{2,1,0:T(1,128)S(1)} collective-permute-done((f32[1,1,2048]{2,1,0:T(1,128)S(1)}, f32[1,1,2048]{2,1,0:T(1,128)S(1)}, u32[]{:S(2)}, u32[]{:S(2)}) %collective-permute-start.11) | collective-permute-done | bytes 8224 | tf_op jit(solution)/shard_map/ppermute | solution.py:373
  42.7 2.4 %shard_map.82 = (f32[1,2048]{1,0:T(1,128)S(1)}, f32[1024,2048]{1,0:T(8,128)S(1)}, f32[1,1,1024]{2,1,0:T(1,128)S(1)}) custom-call(f32[1024,2048]{1,0:T(8,128)S(1)} %get-tuple-element.39.s_ref, f32[1,2048]{1,0:T(1,128)S(1)} %bitcast.6, f32[1,1024]{1,0:T(1,128)S(1)} %get-tuple-element.42.f_ref, f32[1024,128]{1,0:T(8,128)S(1)} %get-tuple-element.43.wide_ref, ...), custom_call_target="tpu_custom_call" | custom-call | tf_op jit(solution)/shard_map/pallas_call | solution.py:354
  45.1 2.1 %collective-permute-start.12 = (f32[1,1,1024]{2,1,0:T(1,128)S(1)}, f32[1,1,1024]{2,1,0:T(1,128)S(1)}, u32[]{:S(2)}, u32[]{:S(2)}) collective-permute-start(f32[1,1,1024]{2,1,0:T(1,128)S(1)} %get-tuple-element.47.refs_0_), channel_id=1, source_target_pairs={{0,1},{1,0},{2,3},{3,2},{4,5},{5,4},{6,7},{7,6},{8,9},{9,8},{10,11... | collective-permute-start | bytes 12296 | tf_op jit(solution)/shard_map/ppermute | solution.py:373
  50.4 2.1 %collective-permute-done.13.refs_1_ = f32[1,1,1024]{2,1,0:T(1,128)S(1)} collective-permute-done((f32[1,1,1024]{2,1,0:T(1,128)S(1)}, f32[1,1,1024]{2,1,0:T(1,128)S(1)}, u32[]{:S(2)}, u32[]{:S(2)}) %collective-permute-start.13) | collective-permute-done | bytes 4128 | tf_op jit(solution)/shard_map/ppermute | solution.py:373
  52.5 3.9 %shard_map.84.refs_0_ = f32[1,1,2048]{2,1,0:T(1,128)S(1)} custom-call(f32[1024,2048]{1,0:T(8,128)S(1)} %get-tuple-element.39.s_ref, f32[1024,2048]{1,0:T(8,128)S(1)} %get-tuple-element.45.p_ref, f32[1,1024]{1,0:T(1,128)S(1)} %get-tuple-element.40.mass_ref, f32[1,1024]{1,0:T(1,128)S(1)} %get-tuple-element.42.f_ref, f32[1,2048]{1,0:T(1,128)S(1)} %get-tuple-element.46.g_ref, ...), custom_call_target="tpu_custom_call" | custom-call | tf_op jit(solution)/shard_map/pallas_call | solution.py:354
  57.7 3.6 %collective-permute-done.15.refs_1_ = f32[1,1,2048]{2,1,0:T(1,128)S(1)} collective-permute-done((f32[1,1,2048]{2,1,0:T(1,128)S(1)}, f32[1,1,2048]{2,1,0:T(1,128)S(1)}, u32[]{:S(2)}, u32[]{:S(2)}) %collective-permute-start.15) | collective-permute-done | bytes 8224 | tf_op jit(solution)/shard_map/ppermute | solution.py:373
  61.3 1.8 %collective-permute-start.16 = (f32[1,1,2048]{2,1,0:T(1,128)S(1)}, f32[1,1,2048]{2,1,0:T(1,128)S(1)}, u32[]{:S(2)}, u32[]{:S(2)}) collective-permute-start(f32[1,1,2048]{2,1,0:T(1,128)S(1)} %shard_map.86.refs_0_), channel_id=1, source_target_pairs={{0,16},{4,20},{8,24},{12,28},{16,0},{20,4},{24,8},{28,12},{1,17},{... | collective-permute-start | bytes 24584 | tf_op jit(solution)/shard_map/ppermute | solution.py:373
  63.1 2.9 %collective-permute-done.16.refs_1_ = f32[1,1,2048]{2,1,0:T(1,128)S(1)} collective-permute-done((f32[1,1,2048]{2,1,0:T(1,128)S(1)}, f32[1,1,2048]{2,1,0:T(1,128)S(1)}, u32[]{:S(2)}, u32[]{:S(2)}) %collective-permute-start.16) | collective-permute-done | bytes 8224 | tf_op jit(solution)/shard_map/ppermute | solution.py:373
  67.2 2.1 %collective-permute-start.17 = (f32[1,1,1024]{2,1,0:T(1,128)S(1)}, f32[1,1,1024]{2,1,0:T(1,128)S(1)}, u32[]{:S(2)}, u32[]{:S(2)}) collective-permute-start(f32[1,1,1024]{2,1,0:T(1,128)S(1)} %shard_map.87.refs_0_), channel_id=1, source_target_pairs={{0,1},{1,0},{2,3},{3,2},{4,5},{5,4},{6,7},{7,6},{8,9},{9,8},{10,11... | collective-permute-start | bytes 12296 | tf_op jit(solution)/shard_map/ppermute | solution.py:373
  72.5 2.1 %collective-permute-done.18.refs_1_ = f32[1,1,1024]{2,1,0:T(1,128)S(1)} collective-permute-done((f32[1,1,1024]{2,1,0:T(1,128)S(1)}, f32[1,1,1024]{2,1,0:T(1,128)S(1)}, u32[]{:S(2)}, u32[]{:S(2)}) %collective-permute-start.18) | collective-permute-done | bytes 4128 | tf_op jit(solution)/shard_map/ppermute | solution.py:373
  74.6 3.9 %shard_map.89 = (f32[1,1024]{1,0:T(1,128)S(1)}, f32[1,1,2048]{2,1,0:T(1,128)S(1)}) custom-call(f32[1024,2048]{1,0:T(8,128)S(1)} %get-tuple-element.39.s_ref, f32[1024,2048]{1,0:T(8,128)S(1)} %get-tuple-element.45.p_ref, f32[1,1024]{1,0:T(1,128)S(1)} %get-tuple-element.40.mass_ref, f32[1,1024]{1,0:T(1,128)S(1)} %get-tuple-element.42.f_ref, ...), custom_call_target="tpu_custom_call" | custom-call | tf_op jit(solution)/shard_map/pallas_call | solution.py:354
  80.6 2.9 %collective-permute-done.20.refs_1_ = f32[1,1,2048]{2,1,0:T(1,128)S(1)} collective-permute-done((f32[1,1,2048]{2,1,0:T(1,128)S(1)}, f32[1,1,2048]{2,1,0:T(1,128)S(1)}, u32[]{:S(2)}, u32[]{:S(2)}) %collective-permute-start.20) | collective-permute-done | bytes 8224 | tf_op jit(solution)/shard_map/ppermute | solution.py:373
  83.5 1.8 %collective-permute-start.21 = (f32[1,1,2048]{2,1,0:T(1,128)S(1)}, f32[1,1,2048]{2,1,0:T(1,128)S(1)}, u32[]{:S(2)}, u32[]{:S(2)}) collective-permute-start(f32[1,1,2048]{2,1,0:T(1,128)S(1)} %shard_map.91.refs_0_), channel_id=1, source_target_pairs={{0,16},{4,20},{8,24},{12,28},{16,0},{20,4},{24,8},{28,12},{1,17},{... | collective-permute-start | bytes 24584 | tf_op jit(solution)/shard_map/ppermute | solution.py:373
  85.2 2.9 %collective-permute-done.21.refs_1_ = f32[1,1,2048]{2,1,0:T(1,128)S(1)} collective-permute-done((f32[1,1,2048]{2,1,0:T(1,128)S(1)}, f32[1,1,2048]{2,1,0:T(1,128)S(1)}, u32[]{:S(2)}, u32[]{:S(2)}) %collective-permute-start.21) | collective-permute-done | bytes 8224 | tf_op jit(solution)/shard_map/ppermute | solution.py:373
  88.1 6.1 %shard_map.92 = (f32[1,1024]{1,0:T(1,128)}, f32[1,2048]{1,0:T(1,128)}, f32[136,128]{1,0:T(8,128)S(1)}, f32[136,128]{1,0:T(8,128)S(1)}, f32[136,128]{1,0:T(8,128)S(1)}, /*index=5*/f32[136,128]{1,0:T(8,128)S(1)}) custom-call(s32[1]{0:T(128)} %bitcast.me_ref, f32[1024,2048]{1,0:T(8,128)S(1)} %get-tuple-element.39.s_ref, ...), custom_call_target="tpu_custom_call" | custom-call | tf_op jit(solution)/shard_map/pallas_call | solution.py:354
  94.2 2.1 %collective-permute-start.22 = (f32[136,128]{1,0:T(8,128)S(1)}, f32[136,128]{1,0:T(8,128)S(1)}, u32[]{:S(2)}, u32[]{:S(2)}) collective-permute-start(f32[136,128]{1,0:T(8,128)S(1)} %get-tuple-element.56), channel_id=1, source_target_pairs={{0,1},{1,2},{2,3},{3,0},{4,5},{5,6},{6,7},{7,4},{8,9},{9,10},{10,1... | collective-permute-start | bytes 208904 | tf_op jit(solution)/shard_map/ppermute | solution.py:369
  (53 shorter events, 32.1 us)
Async XLA Ops:
  0.6 8.9 %collective-permute-start.1 = (f32[8,2048]{1,0:T(8,128)}, f32[8,2048]{1,0:T(8,128)S(1)}, u32[]{:S(2)}, u32[]{:S(2)}) collective-permute-start(f32[8,2048]{1,0:T(8,128)} %param.6), channel_id=1, source_target_pairs={{0,16},{4,20},{8,24},{12,28},{16,0},{20,4},{24,8},{28,12},{1,17},{... | collective-permute-start | bytes 196616 | tf_op jit(solution)/shard_map/ppermute | solution.py:373
  4.7 4.8 %collective-permute-start = (f32[8,2048]{1,0:T(8,128)}, f32[8,2048]{1,0:T(8,128)S(1)}, u32[]{:S(2)}, u32[]{:S(2)}) collective-permute-start(f32[8,2048]{1,0:T(8,128)} %param.6), channel_id=1, source_target_pairs={{0,8},{4,12},{8,0},{12,4},{16,24},{20,28},{24,16},{28,20},{1,9},{5... | collective-permute-start | bytes 196616 | tf_op jit(solution)/shard_map/ppermute | solution.py:373
  6.3 6.3 %collective-permute-start.2 = (f32[8,2048]{1,0:T(8,128)}, f32[8,2048]{1,0:T(8,128)S(1)}, u32[]{:S(2)}, u32[]{:S(2)}) collective-permute-start(f32[8,2048]{1,0:T(8,128)} %param.6), channel_id=1, source_target_pairs={{0,24},{4,28},{8,16},{12,20},{16,8},{20,12},{24,0},{28,4},{1,25},{... | collective-permute-start | bytes 196616 | tf_op jit(solution)/shard_map/ppermute | solution.py:373
  6.3 7.1 %collective-permute-start.4 = (f32[16,1024]{1,0:T(8,128)}, f32[16,1024]{1,0:T(8,128)S(1)}, u32[]{:S(2)}, u32[]{:S(2)}) collective-permute-start(f32[16,1024]{1,0:T(8,128)} %x_ref), channel_id=1, source_target_pairs={{0,2},{1,3},{2,0},{3,1},{4,6},{5,7},{6,4},{7,5},{8,10},{9,11},{10,... | collective-permute-start | bytes 196616 | tf_op jit(solution)/shard_map/ppermute | solution.py:369
  8.1 5.4 %collective-permute-start.3 = (f32[16,1024]{1,0:T(8,128)}, f32[16,1024]{1,0:T(8,128)S(1)}, u32[]{:S(2)}, u32[]{:S(2)}) collective-permute-start(f32[16,1024]{1,0:T(8,128)} %x_ref), channel_id=1, source_target_pairs={{0,1},{1,2},{2,3},{3,0},{4,5},{5,6},{6,7},{7,4},{8,9},{9,10},{10,1... | collective-permute-start | bytes 196616 | tf_op jit(solution)/shard_map/ppermute | solution.py:369
  13.5 4.9 %collective-permute-start.6 = (f32[32,2048]{1,0:T(8,128)S(1)}, f32[32,2048]{1,0:T(8,128)S(1)}, u32[]{:S(2)}, u32[]{:S(2)}) collective-permute-start(f32[32,2048]{1,0:T(8,128)S(1)} %pad_maximum_fusion.refs_4_), channel_id=1, source_target_pairs={{0,4},{4,0},{8,12},{12,8},{16,20},{20,16},{24,28},{28,24},{1,5},{5... | collective-permute-start | bytes 786440 | tf_op jit(solution)/shard_map/ppermute | solution.py:373
  13.6 4.8 %collective-permute-start.5 = (f32[16,1024]{1,0:T(8,128)}, f32[16,1024]{1,0:T(8,128)S(1)}, u32[]{:S(2)}, u32[]{:S(2)}) collective-permute-start(f32[16,1024]{1,0:T(8,128)} %x_ref), channel_id=1, source_target_pairs={{0,3},{1,0},{2,1},{3,2},{4,7},{5,4},{6,5},{7,6},{8,11},{9,8},{10,9... | collective-permute-start | bytes 196616 | tf_op jit(solution)/shard_map/ppermute | solution.py:369
  22.9 3.9 %collective-permute-start.7 = (f32[1,1,1024]{2,1,0:T(1,128)S(1)}, f32[1,1,1024]{2,1,0:T(1,128)S(1)}, u32[]{:S(2)}, u32[]{:S(2)}) collective-permute-start(f32[1,1,1024]{2,1,0:T(1,128)S(1)} %get-tuple-element.41.refs_0_), channel_id=1, source_target_pairs={{0,1},{1,0},{2,3},{3,2},{4,5},{5,4},{6,7},{7,6},{8,9},{9,8},{10,11... | collective-permute-start | bytes 12296 | tf_op jit(solution)/shard_map/ppermute | solution.py:373
  26.8 3.7 %collective-permute-start.8 = (f32[1,1,1024]{2,1,0:T(1,128)S(1)}, f32[1,1,1024]{2,1,0:T(1,128)S(1)}, u32[]{:S(2)}, u32[]{:S(2)}) collective-permute-start(f32[1,1,1024]{2,1,0:T(1,128)S(1)} %shard_map.78.refs_0_), channel_id=1, source_target_pairs={{0,2},{1,3},{2,0},{3,1},{4,6},{5,7},{6,4},{7,5},{8,10},{9,11},{10,... | collective-permute-start | bytes 12296 | tf_op jit(solution)/shard_map/ppermute | solution.py:373
  33.1 1.2 %collective-permute-start.9 = (f32[1,1,2048]{2,1,0:T(1,128)S(1)}, f32[1,1,2048]{2,1,0:T(1,128)S(1)}, u32[]{:S(2)}, u32[]{:S(2)}) collective-permute-start(f32[1,1,2048]{2,1,0:T(1,128)S(1)} %get-tuple-element.44.refs_0_), channel_id=1, source_target_pairs={{0,4},{4,0},{8,12},{12,8},{16,20},{20,16},{24,28},{28,24},{1,5},{5... | collective-permute-start | bytes 24584 | tf_op jit(solution)/shard_map/ppermute | solution.py:373
  34.4 3.7 %collective-permute-start.10 = (f32[1,1,2048]{2,1,0:T(1,128)S(1)}, f32[1,1,2048]{2,1,0:T(1,128)S(1)}, u32[]{:S(2)}, u32[]{:S(2)}) collective-permute-start(f32[1,1,2048]{2,1,0:T(1,128)S(1)} %shard_map.80.refs_0_), channel_id=1, source_target_pairs={{0,8},{4,12},{8,0},{12,4},{16,24},{20,28},{24,16},{28,20},{1,9},{5... | collective-permute-start | bytes 24584 | tf_op jit(solution)/shard_map/ppermute | solution.py:373
  38.1 4.6 %collective-permute-start.11 = (f32[1,1,2048]{2,1,0:T(1,128)S(1)}, f32[1,1,2048]{2,1,0:T(1,128)S(1)}, u32[]{:S(2)}, u32[]{:S(2)}) collective-permute-start(f32[1,1,2048]{2,1,0:T(1,128)S(1)} %shard_map.81.refs_0_), channel_id=1, source_target_pairs={{0,16},{4,20},{8,24},{12,28},{16,0},{20,4},{24,8},{28,12},{1,17},{... | collective-permute-start | bytes 24584 | tf_op jit(solution)/shard_map/ppermute | solution.py:373
  45.1 3.7 %collective-permute-start.12 = (f32[1,1,1024]{2,1,0:T(1,128)S(1)}, f32[1,1,1024]{2,1,0:T(1,128)S(1)}, u32[]{:S(2)}, u32[]{:S(2)}) collective-permute-start(f32[1,1,1024]{2,1,0:T(1,128)S(1)} %get-tuple-element.47.refs_0_), channel_id=1, source_target_pairs={{0,1},{1,0},{2,3},{3,2},{4,5},{5,4},{6,7},{7,6},{8,9},{9,8},{10,11... | collective-permute-start | bytes 12296 | tf_op jit(solution)/shard_map/ppermute | solution.py:373
  48.8 3.7 %collective-permute-start.13 = (f32[1,1,1024]{2,1,0:T(1,128)S(1)}, f32[1,1,1024]{2,1,0:T(1,128)S(1)}, u32[]{:S(2)}, u32[]{:S(2)}) collective-permute-start(f32[1,1,1024]{2,1,0:T(1,128)S(1)} %shard_map.83.refs_0_), channel_id=1, source_target_pairs={{0,2},{1,3},{2,0},{3,1},{4,6},{5,7},{6,4},{7,5},{8,10},{9,11},{10,... | collective-permute-start | bytes 12296 | tf_op jit(solution)/shard_map/ppermute | solution.py:373
  56.4 1.2 %collective-permute-start.14 = (f32[1,1,2048]{2,1,0:T(1,128)S(1)}, f32[1,1,2048]{2,1,0:T(1,128)S(1)}, u32[]{:S(2)}, u32[]{:S(2)}) collective-permute-start(f32[1,1,2048]{2,1,0:T(1,128)S(1)} %shard_map.84.refs_0_), channel_id=1, source_target_pairs={{0,4},{4,0},{8,12},{12,8},{16,20},{20,16},{24,28},{28,24},{1,5},{5... | collective-permute-start | bytes 24584 | tf_op jit(solution)/shard_map/ppermute | solution.py:373
  57.6 3.7 %collective-permute-start.15 = (f32[1,1,2048]{2,1,0:T(1,128)S(1)}, f32[1,1,2048]{2,1,0:T(1,128)S(1)}, u32[]{:S(2)}, u32[]{:S(2)}) collective-permute-start(f32[1,1,2048]{2,1,0:T(1,128)S(1)} %shard_map.85.refs_0_), channel_id=1, source_target_pairs={{0,8},{4,12},{8,0},{12,4},{16,24},{20,28},{24,16},{28,20},{1,9},{5... | collective-permute-start | bytes 24584 | tf_op jit(solution)/shard_map/ppermute | solution.py:373
  61.3 4.6 %collective-permute-start.16 = (f32[1,1,2048]{2,1,0:T(1,128)S(1)}, f32[1,1,2048]{2,1,0:T(1,128)S(1)}, u32[]{:S(2)}, u32[]{:S(2)}) collective-permute-start(f32[1,1,2048]{2,1,0:T(1,128)S(1)} %shard_map.86.refs_0_), channel_id=1, source_target_pairs={{0,16},{4,20},{8,24},{12,28},{16,0},{20,4},{24,8},{28,12},{1,17},{... | collective-permute-start | bytes 24584 | tf_op jit(solution)/shard_map/ppermute | solution.py:373
  67.2 3.7 %collective-permute-start.17 = (f32[1,1,1024]{2,1,0:T(1,128)S(1)}, f32[1,1,1024]{2,1,0:T(1,128)S(1)}, u32[]{:S(2)}, u32[]{:S(2)}) collective-permute-start(f32[1,1,1024]{2,1,0:T(1,128)S(1)} %shard_map.87.refs_0_), channel_id=1, source_target_pairs={{0,1},{1,0},{2,3},{3,2},{4,5},{5,4},{6,7},{7,6},{8,9},{9,8},{10,11... | collective-permute-start | bytes 12296 | tf_op jit(solution)/shard_map/ppermute | solution.py:373
  70.9 3.7 %collective-permute-start.18 = (f32[1,1,1024]{2,1,0:T(1,128)S(1)}, f32[1,1,1024]{2,1,0:T(1,128)S(1)}, u32[]{:S(2)}, u32[]{:S(2)}) collective-permute-start(f32[1,1,1024]{2,1,0:T(1,128)S(1)} %shard_map.88.refs_0_), channel_id=1, source_target_pairs={{0,2},{1,3},{2,0},{3,1},{4,6},{5,7},{6,4},{7,5},{8,10},{9,11},{10,... | collective-permute-start | bytes 12296 | tf_op jit(solution)/shard_map/ppermute | solution.py:373
  79.7 3.7 %collective-permute-start.20 = (f32[1,1,2048]{2,1,0:T(1,128)S(1)}, f32[1,1,2048]{2,1,0:T(1,128)S(1)}, u32[]{:S(2)}, u32[]{:S(2)}) collective-permute-start(f32[1,1,2048]{2,1,0:T(1,128)S(1)} %shard_map.90.refs_0_), channel_id=1, source_target_pairs={{0,8},{4,12},{8,0},{12,4},{16,24},{20,28},{24,16},{28,20},{1,9},{5... | collective-permute-start | bytes 24584 | tf_op jit(solution)/shard_map/ppermute | solution.py:373
  83.5 4.6 %collective-permute-start.21 = (f32[1,1,2048]{2,1,0:T(1,128)S(1)}, f32[1,1,2048]{2,1,0:T(1,128)S(1)}, u32[]{:S(2)}, u32[]{:S(2)}) collective-permute-start(f32[1,1,2048]{2,1,0:T(1,128)S(1)} %shard_map.91.refs_0_), channel_id=1, source_target_pairs={{0,16},{4,20},{8,24},{12,28},{16,0},{20,4},{24,8},{28,12},{1,17},{... | collective-permute-start | bytes 24584 | tf_op jit(solution)/shard_map/ppermute | solution.py:373
  94.2 5.3 %collective-permute-start.22 = (f32[136,128]{1,0:T(8,128)S(1)}, f32[136,128]{1,0:T(8,128)S(1)}, u32[]{:S(2)}, u32[]{:S(2)}) collective-permute-start(f32[136,128]{1,0:T(8,128)S(1)} %get-tuple-element.56), channel_id=1, source_target_pairs={{0,1},{1,2},{2,3},{3,0},{4,5},{5,6},{6,7},{7,4},{8,9},{9,10},{10,1... | collective-permute-start | bytes 208904 | tf_op jit(solution)/shard_map/ppermute | solution.py:369
  96.3 4.3 %collective-permute-start.23 = (f32[136,128]{1,0:T(8,128)S(1)}, f32[136,128]{1,0:T(8,128)S(1)}, u32[]{:S(2)}, u32[]{:S(2)}) collective-permute-start(f32[136,128]{1,0:T(8,128)S(1)} %get-tuple-element.57), channel_id=1, source_target_pairs={{0,2},{1,3},{2,0},{3,1},{4,6},{5,7},{6,4},{7,5},{8,10},{9,11},{10,... | collective-permute-start | bytes 208904 | tf_op jit(solution)/shard_map/ppermute | solution.py:369
  97.8 4.3 %collective-permute-start.24 = (f32[136,128]{1,0:T(8,128)S(1)}, f32[136,128]{1,0:T(8,128)S(1)}, u32[]{:S(2)}, u32[]{:S(2)}) collective-permute-start(f32[136,128]{1,0:T(8,128)S(1)} %get-tuple-element.58), channel_id=1, source_target_pairs={{0,3},{1,0},{2,1},{3,2},{4,7},{5,4},{6,5},{7,6},{8,11},{9,8},{10,9... | collective-permute-start | bytes 208904 | tf_op jit(solution)/shard_map/ppermute | solution.py:369
  (5 other events, 45.6 us)
where the time goes:
time: 103 us
  waiting for transfers between devices  39.5 us (38%)
  starting transfers between devices  34 us (33%)
  Pallas kernels  25.5 us (25%)
  local copies, waits for them, and re-layouts  2.26 us (2%)
    ppermute x19, waiting for transfers between devices, flip(): return lax.ppermute(v, axis, [(i, i ^ bit) for i in range(size)])  36 us
    pallas_call x18, Pallas kernels, call(): pl.pallas_call(kernel, out_shape=[o if isinstance(o, jax.ShapeDtypeStruct...  25.5 us
    ppermute x19, starting transfers between devices, flip(): return lax.ppermute(v, axis, [(i, i ^ bit) for i in range(size)])  23.7 us
    ppermute x6, starting transfers between devices, turn(): return lax.ppermute(v, axis, [(i, (i + d) % size) for i in range(size)])  10.2 us
    ppermute x6, waiting for transfers between devices, turn(): return lax.ppermute(v, axis, [(i, (i + d) % size) for i in range(size)])  3.43 us
    unnamed x8, local copies, waits for them, and re-layouts  2.26 us
  transfers between devices with their start and end apart: 25, of which 19 were waited for; matrix products, arithmetic and copies ran while one was open for 1% of the time, Pallas kernels for 0%

commit v1 on v0

--- a/solution.py
+++ b/solution.py
@@ -189,41 +189,42 @@
 
 
 def src_first_kernel(count, s_ref, mass_ref, *refs):
-    parts, (f_ref, wide_ref, l_ref) = refs[:count], refs[count:]
+    parts, (f_ref, p_ref, top_ref, l_ref, wide) = refs[:count], refs[count:]
     f = mass_ref[...] - whole_log_sum(parts)
     f_ref[...] = f
-    across(f, wide_ref)
-    repeat(cols_log_sum(s_ref, wide_ref), l_ref)
-
-
-def tgt_first_kernel(count, s_ref, mass_ref, f_ref, wide_ref, *refs):
-    parts, (g_ref, p_ref, l_ref, top_ref, sum_ref) = refs[:count], refs[count:]
+    across(f, wide)
     n, width = s_ref.shape
-    g = jnp.log2(mass_ref[...]) - whole_log_sum(parts)
-    g_ref[...] = g
-    g8 = jnp.broadcast_to(g, (8, width))
-
-    def strip(k, _):
-        rows = eight(k)
-        f = wide_ref[rows, :]
+    cols = width // LANES
+
+    def load(k):
+        rows = eight(k)
+        f = wide[rows, :]
+        return [s_ref[rows, chunk(c)] + f for c in range(cols)]
+
+    def find(k, top):
+        return tuple(jnp.maximum(t, v) for t, v in zip(top, load(k)))
+
+    tops = lax.fori_loop(1, n // 8, find, tuple(load(0)), unroll=4)
+    top = jnp.concatenate([jnp.max(t, axis=0, keepdims=True) for t in tops], axis=1)
+    top8 = jnp.broadcast_to(top, (8, width))
+
+    def add(k, total):
+        rows = eight(k)
         out = []
-        for c in range(width // LANES):
-            p = jnp.exp2((s_ref[rows, chunk(c)] + f) + g8[:, c * LANES : (c + 1) * LANES])
-            p_ref[rows, chunk(c)] = p
-            out.append(p)
-        sum_ref[rows, :] = tree(jnp.add, out)
-        return 0
-
-    lax.fori_loop(0, n // 8, strip, 0, unroll=4)
-    total = to_row(sum_ref[...])
-    l_ref[0] = jnp.log2(total)
-
-    @pl.when(jnp.logical_not(jnp.min(total) >= LOW))
-    def _():
-        l_ref[0] = f_ref[...] + rows_log_sum(s_ref, g, top_ref, sum_ref)
-
-
-def src_kernel(count, s_ref, p_ref, mass_ref, f_ref, g_ref, *refs):
+        for c, (a, v) in enumerate(zip(total, load(k))):
+            e = jnp.exp2(v - top8[:, c * LANES : (c + 1) * LANES])
+            p_ref[rows, chunk(c)] = e
+            out.append(a + e)
+        return tuple(out)
+
+    zero = tuple(jnp.zeros((8, LANES), F32) for _ in range(cols))
+    sums = lax.fori_loop(0, n // 8, add, zero, unroll=4)
+    total = jnp.concatenate([jnp.sum(a, axis=0, keepdims=True) for a in sums], axis=1)
+    top_ref[...] = top
+    repeat(top + jnp.log2(total), l_ref)
+
+
+def src_kernel(count, s_ref, p_ref, mass_ref, f_ref, g_ref, w_ref, *refs):
     parts, (*u_refs, l_ref, wide) = refs[:count], refs[count:]
     n, width = p_ref.shape
     cols = width // LANES
@@ -241,7 +242,7 @@
     zero = tuple(jnp.zeros((8, LANES), F32) for _ in range(cols))
     parts = lax.fori_loop(0, n // 8, add, zero, unroll=4)
     total = jnp.concatenate([jnp.sum(a, axis=0, keepdims=True) for a in parts], axis=1)
-    repeat(jnp.log2(total), l_ref)
+    repeat(jnp.log2(total) + w_ref[...], l_ref)
     fine = jnp.logical_and(jnp.min(total) >= LOW, jnp.max(u) <= HIGH)
 
     @pl.when(jnp.logical_not(fine))
@@ -250,11 +251,22 @@
         repeat(g_ref[...] + cols_log_sum(s_ref, wide), l_ref)
 
 
-def tgt_kernel(count, s_ref, p_ref, mass_ref, f_ref, g_ref, *refs):
-    parts, (l_ref, top_ref, sum_ref) = refs[:count], refs[count:]
+def tgt_kernel(first, count, s_ref, p_ref, mass_ref, f_ref, *refs):
+    if first:
+        top_ref, *refs = refs
+        parts, (g_ref, w_ref, l_ref, top8_ref, sum_ref) = refs[:count], refs[count:]
+        g = jnp.log2(mass_ref[...]) - whole_log_sum(parts)
+        g_ref[...] = g
+        w = g + top_ref[...]
+        w_ref[...] = w
+    else:
+        g_ref, w_ref, *refs = refs
+        parts, (l_ref, top8_ref, sum_ref) = refs[:count], refs[count:]
+        change = jnp.log2(mass_ref[...]) - whole_log_sum(parts)
+        g = g_ref[...] + change
+        w = w_ref[...] + change
     n, width = p_ref.shape
-    change = jnp.log2(mass_ref[...]) - whole_log_sum(parts)
-    v = jnp.exp2(change)
+    v = jnp.exp2(w)
     v8 = jnp.broadcast_to(v, (8, width))
 
     def strip(k, _):
@@ -271,10 +283,10 @@
 
     @pl.when(jnp.logical_not(fine))
     def _():
-        l_ref[0] = f_ref[...] + rows_log_sum(s_ref, g_ref[...] + change, top_ref, sum_ref)
-
-
-def last_kernel(count, me_ref, s_ref, p_ref, mass_ref, f_ref, g_ref, u_ref, xn_ref, yn_ref, y_ref, *refs):
+        l_ref[0] = f_ref[...] + rows_log_sum(s_ref, g, top8_ref, sum_ref)
+
+
+def last_kernel(count, me_ref, s_ref, p_ref, mass_ref, f_ref, g_ref, w_ref, u_ref, xn_ref, yn_ref, y_ref, *refs):
     parts, refs = refs[:count], refs[count:]
     sp_any, tp_any, outs = refs[0], refs[1], refs[2:-7]
     sp, tp, yw, acc, flat, wide, sem = refs[-7:]
@@ -292,7 +304,7 @@
     for copy in copies:
         copy.start()
     u = jnp.exp2(u_ref[...])
-    v = jnp.exp2(change)
+    v = jnp.exp2(w_ref[...] + change)
     step = 256
 
     def project(weight, scale, rescale):
@@ -374,19 +386,17 @@
 
 
 def join_rows(v, axis, size):
-    if spread(size) > 1:
+    if spread(axis, size) > 1:
         return [lax.all_to_all(v, axis, 0, 0, tiled=True)]
-    parts, bit = [v], 1
-    while bit < size:
-        if bit > 1:
-            parts = call(sum_kernel, [v.shape], [], put(*parts))
-        parts = [parts[0], flip(parts[0], axis, size, bit)]
-        bit *= 2
-    return parts
-
-
-def spread(size):
-    return 1 if size in (2, 4, 8) else size
+    if axis == "tgt":
+        return [v] + [turn(v, axis, size, d) for d in range(1, size)]
+    if size > 2:
+        (v,) = call(sum_kernel, [v.shape], [], put(v, *[turn(v, axis, size, d) for d in range(2, size, 2)]))
+    return [v, flip(v, axis, size, 1)]
+
+
+def spread(axis, size):
+    return 1 if size in ((2, 4) if axis == "tgt" else (2, 4, 8)) else size
 
 
 def gather_src(v, size):
@@ -399,9 +409,11 @@
     if v.shape[0] % 8 or size & (size - 1):
         return [lax.all_gather(v, "src", axis=0, tiled=True)], [None], other
     order = list(range(0, size, 2))
-    mine = jnp.concatenate([v] + [flip(v, "src", size, d) for d in order[1:]], axis=0)
-    mine, *early = lax.optimization_barrier([mine] + other[:-1])
-    other = early + other[-1:]
+    far = [flip(v, "src", size, d) for d in order[2:]]
+    again, last = lax.optimization_barrier((v, other[-1]))
+    near = [flip(again, "src", size, d) for d in order[1:2]]
+    mine = jnp.concatenate([v] + near + far, axis=0)
+    mine, *other = lax.optimization_barrier([mine] + other[:-1] + [last])
     return [mine, flip(mine, "src", size, 1)], [order, [d + 1 for d in order]], other
 
 
@@ -411,7 +423,7 @@
     k = own * peers_tgt
     pack = (own + 1) * (n // LANES)
     row, col = (1, n), (1, width)
-    rows, cols = (spread(peers_tgt), 1, n), (spread(peers_src), 1, width)
+    rows, cols = (spread("tgt", peers_tgt), 1, n), (spread("src", peers_src), 1, width)
     lane = pltpu.VMEM((n, LANES), F32)
     me = lax.axis_index(("src", "tgt")).astype(jnp.int32).reshape(1)
     xs, xplan = gather_src(src_pts, peers_tgt)
@@ -426,15 +438,15 @@
         [(SMEM, me)] + put(pot, x, *xs[1:], *ys),
     )
     parts = join_rows(l, "tgt", peers_tgt)
-    f, wide, l = call(
-        functools.partial(src_first_kernel, len(parts)), [row, (n, LANES), cols], [], put(s, sm, *parts)
+    f, p, top, l = call(
+        functools.partial(src_first_kernel, len(parts)), [row, (n, width), col, cols], [lane], put(s, sm, *parts)
     )
     parts = join_rows(l, "src", peers_src)
-    g, p, l = call(
-        functools.partial(tgt_first_kernel, len(parts)),
-        [col, (n, width), rows],
+    g, w, l = call(
+        functools.partial(tgt_kernel, True, len(parts)),
+        [col, col, rows],
         [lane, lane],
-        put(s, tm, f, wide, *parts),
+        put(s, p, tm, f, top, *parts),
     )
     for step in range(1, ITERS):
         parts = join_rows(l, "tgt", peers_tgt)
@@ -442,11 +454,16 @@
             functools.partial(src_kernel, len(parts)),
             [row, cols] if step == ITERS - 1 else [cols],
             [lane],
-            put(s, p, sm, f, g, *parts),
+            put(s, p, sm, f, g, w, *parts),
         )
         parts = join_rows(l, "src", peers_src)
         if step < ITERS - 1:
-            (l,) = call(functools.partial(tgt_kernel, len(parts)), [rows], [lane, lane], put(s, p, tm, f, g, *parts))
+            (l,) = call(
+                functools.partial(tgt_kernel, False, len(parts)),
+                [rows],
+                [lane, lane],
+                put(s, p, tm, f, g, w, *parts),
+            )
     src_pot, tgt_pot, *blocks = call(
         functools.partial(last_kernel, len(parts)),
         [row, col] + [(pack, LANES)] * peers_tgt,
@@ -459,7 +476,7 @@
             lane,
             pltpu.SemaphoreType.DMA((2,)),
         ],
-        [(SMEM, me)] + put(s, p, tm, f, g, *u, xn, yn, yo, *parts),
+        [(SMEM, me)] + put(s, p, tm, f, g, w, *u, xn, yn, yo, *parts),
         [HBM, HBM] + [VMEM] * peers_tgt,
     )
     came = [blocks[0]] + [turn(blocks[d], "tgt", peers_tgt, d) for d in range(1, peers_tgt)]

time: 103 us -> 90.8 us (0.88)
  waiting for transfers between devices: 39.5 us -> 30.7 us
  Pallas kernels: 25.5 us -> 21.5 us
    ppermute x19 -> x7, waiting for transfers between devices: 36 us -> 5.08 us  [flip(): return lax.ppermute(v, axis, [(i, i ^ bit) for i in range(size)])]
    ppermute x6 -> x24, waiting for transfers between devices: 3.43 us -> 25.6 us  [turn(): return lax.ppermute(v, axis, [(i, (i + d) % size) for i in range(size)])]
    ppermute x6 -> x24, starting transfers between devices: 10.2 us -> 30.1 us  [turn(): return lax.ppermute(v, axis, [(i, (i + d) % size) for i in range(size)])]
    ppermute x19 -> x7, starting transfers between devices: 23.7 us -> 4.39 us  [flip(): return lax.ppermute(v, axis, [(i, i ^ bit) for i in range(size)])]
    pallas_call x18 -> x12, Pallas kernels: 25.5 us -> 21.5 us  [call(): pl.pallas_call(kernel, out_shape=[o if isinstance(o, jax.ShapeDtypeStruct...]
  transfers between devices with their start and end apart: 25 -> 31, of which waited for: 19 -> 23; matrix products, arithmetic and copies ran while one was open for 1% -> 1% of each run, Pallas kernels for 0% -> 0%
where the time goes in v1:
time: 90.8 us; the launch traced here: 90.5 us
  starting transfers between devices  34.5 us (38%)
  waiting for transfers between devices  30.7 us (34%)
  Pallas kernels  21.5 us (24%)
  local copies, waits for them, and re-layouts  2.23 us (2%)
    ppermute x24, starting transfers between devices, turn(): return lax.ppermute(v, axis, [(i, (i + d) % size) for i in range(size)])  30.1 us
    ppermute x24, waiting for transfers between devices, turn(): return lax.ppermute(v, axis, [(i, (i + d) % size) for i in range(size)])  25.6 us
    pallas_call x12, Pallas kernels, call(): pl.pallas_call(kernel, out_shape=[o if isinstance(o, jax.ShapeDtypeStruct...  21.5 us
    ppermute x7, waiting for transfers between devices, flip(): return lax.ppermute(v, axis, [(i, i ^ bit) for i in range(size)])  5.08 us
    ppermute x7, starting transfers between devices, flip(): return lax.ppermute(v, axis, [(i, i ^ bit) for i in range(size)])  4.39 us
    unnamed x8, local copies, waits for them, and re-layouts  2.23 us
  transfers between devices with their start and end apart: 31, of which 23 were waited for; matrix products, arithmetic and copies ran while one was open for 1% of the time, Pallas kernels for 0%

profile of v1, /device:TPU:0, one launch (start us, length us, event | category | flops | bytes accessed | tf_op | source)
XLA Modules:
  0.0 90.5 jit_solution(3404647438897362091)
XLA Ops:
  0.6 3.9 %collective-permute-start = (f32[16,1024]{1,0:T(8,128)}, f32[16,1024]{1,0:T(8,128)S(1)}, u32[]{:S(2)}, u32[]{:S(2)}) collective-permute-start(f32[16,1024]{1,0:T(8,128)} %x_ref), channel_id=1, source_target_pairs={{0,3},{1,0},{2,1},{3,2},{4,7},{5,4},{6,5},{7,6},{8,11},{9,8},{10,9... | collective-permute-start | bytes 196616 | tf_op jit(solution)/shard_map/ppermute | solution.py:381
  4.6 2.6 %collective-permute-start.2 = (f32[8,2048]{1,0:T(8,128)}, f32[8,2048]{1,0:T(8,128)S(1)}, u32[]{:S(2)}, u32[]{:S(2)}) collective-permute-start(f32[8,2048]{1,0:T(8,128)} %param.6), channel_id=1, source_target_pairs={{0,16},{4,20},{8,24},{12,28},{16,0},{20,4},{24,8},{28,12},{1,17},{... | collective-permute-start | bytes 196616 | tf_op jit(solution)/shard_map/ppermute | solution.py:385
  8.8 1.8 %collective-permute-start.4 = (f32[16,1024]{1,0:T(8,128)}, f32[16,1024]{1,0:T(8,128)S(1)}, u32[]{:S(2)}, u32[]{:S(2)}) collective-permute-start(f32[16,1024]{1,0:T(8,128)} %x_ref), channel_id=1, source_target_pairs={{0,1},{1,2},{2,3},{3,0},{4,5},{5,6},{6,7},{7,4},{8,9},{9,10},{10,1... | collective-permute-start | bytes 196616 | tf_op jit(solution)/shard_map/ppermute | solution.py:381
  10.6 1.5 %collective-permute-start.5 = (f32[16,1024]{1,0:T(8,128)}, f32[16,1024]{1,0:T(8,128)S(1)}, u32[]{:S(2)}, u32[]{:S(2)}) collective-permute-start(f32[16,1024]{1,0:T(8,128)} %x_ref), channel_id=1, source_target_pairs={{0,2},{1,3},{2,0},{3,1},{4,6},{5,7},{6,4},{7,5},{8,10},{9,11},{10,... | collective-permute-start | bytes 196616 | tf_op jit(solution)/shard_map/ppermute | solution.py:381
  12.1 1.5 %collective-permute-done.3 = f32[8,2048]{1,0:T(8,128)S(1)} collective-permute-done((f32[8,2048]{1,0:T(8,128)}, f32[8,2048]{1,0:T(8,128)S(1)}, u32[]{:S(2)}, u32[]{:S(2)}) %collective-permute-start.3) | collective-permute-done | bytes 65568 | tf_op jit(solution)/shard_map/ppermute | solution.py:385
  17.3 4.4 %shard_map.77 = (f32[1024,2048]{1,0:T(8,128)S(1)}, f32[1,1,1024]{2,1,0:T(1,128)S(1)}, f32[1,1024]{1,0:T(1,128)S(1)}, f32[1,2048]{1,0:T(1,128)S(1)}, f32[64,2048]{1,0:T(8,128)S(1)}) custom-call(s32[1]{0:T(128)} %bitcast.me_ref, f32[1,2048]{1,0:T(1,128)S(1)} %get-tuple-element.40.pot_ref, f32[16,1024]{1,0:T(8,128)S(1)} %get-tuple-element.41.refs_0_, ...), custom_call_target="tpu_custom_call" | custom-call | tf_op jit(solution)/shard_map/pallas_call | solution.py:366
  23.8 1.5 %collective-permute-start.7 = (f32[1,1,1024]{2,1,0:T(1,128)S(1)}, f32[1,1,1024]{2,1,0:T(1,128)S(1)}, u32[]{:S(2)}, u32[]{:S(2)}) collective-permute-start(f32[1,1,1024]{2,1,0:T(1,128)S(1)} %get-tuple-element.48.refs_0_), channel_id=1, source_target_pairs={{0,1},{1,2},{2,3},{3,0},{4,5},{5,6},{6,7},{7,4},{8,9},{9,10},{10,1... | collective-permute-start | bytes 12296 | tf_op jit(solution)/shard_map/ppermute | solution.py:381
  26.5 1.9 %collective-permute-done.7.refs_1_ = f32[1,1,1024]{2,1,0:T(1,128)S(1)} collective-permute-done((f32[1,1,1024]{2,1,0:T(1,128)S(1)}, f32[1,1,1024]{2,1,0:T(1,128)S(1)}, u32[]{:S(2)}, u32[]{:S(2)}) %collective-permute-start.7) | collective-permute-done | bytes 4128 | tf_op jit(solution)/shard_map/ppermute | solution.py:381
  28.4 2.9 %shard_map.78 = (f32[1,1024]{1,0:T(1,128)S(1)}, f32[1024,2048]{1,0:T(8,128)S(1)}, f32[1,2048]{1,0:T(1,128)S(1)}, f32[1,1,2048]{2,1,0:T(1,128)S(1)}) custom-call(f32[1024,2048]{1,0:T(8,128)S(1)} %get-tuple-element.46.s_ref, f32[1,1024]{1,0:T(1,128)S(1)} %get-tuple-element.47.mass_ref, f32[1,1,1024]{2,1,0:T(1,128)S(1)} %get-tuple-element.48.refs_0_, ...), custom_call_target="tpu_custom_call" | custom-call | tf_op jit(solution)/shard_map/pallas_call | solution.py:366
  31.3 2.5 %collective-permute-start.12 = (f32[1,1,2048]{2,1,0:T(1,128)S(1)}, f32[1,1,2048]{2,1,0:T(1,128)S(1)}, u32[]{:S(2)}, u32[]{:S(2)}) collective-permute-start(f32[1,1,2048]{2,1,0:T(1,128)S(1)} %get-tuple-element.52.refs_0_), channel_id=1, source_target_pairs={{0,24},{4,28},{8,0},{12,4},{16,8},{20,12},{24,16},{28,20},{1,25},{... | collective-permute-start | bytes 24584 | tf_op jit(solution)/shard_map/ppermute | solution.py:381
  34.1 1.8 %collective-permute-start.10 = (f32[1,1,2048]{2,1,0:T(1,128)S(1)}, f32[1,1,2048]{2,1,0:T(1,128)S(1)}, u32[]{:S(2)}, u32[]{:S(2)}) collective-permute-start(f32[1,1,2048]{2,1,0:T(1,128)S(1)} %get-tuple-element.52.refs_0_), channel_id=1, source_target_pairs={{0,8},{4,12},{8,16},{12,20},{16,24},{20,28},{24,0},{28,4},{1,9},{5... | collective-permute-start | bytes 24584 | tf_op jit(solution)/shard_map/ppermute | solution.py:381
  35.9 2.4 %collective-permute-done.11.refs_2_ = f32[1,1,2048]{2,1,0:T(1,128)S(1)} collective-permute-done((f32[1,1,2048]{2,1,0:T(1,128)S(1)}, f32[1,1,2048]{2,1,0:T(1,128)S(1)}, u32[]{:S(2)}, u32[]{:S(2)}) %collective-permute-start.11) | collective-permute-done | bytes 8224 | tf_op jit(solution)/shard_map/ppermute | solution.py:381
  42.6 1.5 %collective-permute-start.15 = (f32[1,1,1024]{2,1,0:T(1,128)S(1)}, f32[1,1,1024]{2,1,0:T(1,128)S(1)}, u32[]{:S(2)}, u32[]{:S(2)}) collective-permute-start(f32[1,1,1024]{2,1,0:T(1,128)S(1)} %get-tuple-element.55.refs_0_), channel_id=1, source_target_pairs={{0,2},{1,3},{2,0},{3,1},{4,6},{5,7},{6,4},{7,5},{8,10},{9,11},{10,... | collective-permute-start | bytes 12296 | tf_op jit(solution)/shard_map/ppermute | solution.py:381
  44.1 1.7 %collective-permute-start.14 = (f32[1,1,1024]{2,1,0:T(1,128)S(1)}, f32[1,1,1024]{2,1,0:T(1,128)S(1)}, u32[]{:S(2)}, u32[]{:S(2)}) collective-permute-start(f32[1,1,1024]{2,1,0:T(1,128)S(1)} %get-tuple-element.55.refs_0_), channel_id=1, source_target_pairs={{0,1},{1,2},{2,3},{3,0},{4,5},{5,6},{6,7},{7,4},{8,9},{9,10},{10,1... | collective-permute-start | bytes 12296 | tf_op jit(solution)/shard_map/ppermute | solution.py:381
  46.2 2.4 %collective-permute-done.14.refs_1_ = f32[1,1,1024]{2,1,0:T(1,128)S(1)} collective-permute-done((f32[1,1,1024]{2,1,0:T(1,128)S(1)}, f32[1,1,1024]{2,1,0:T(1,128)S(1)}, u32[]{:S(2)}, u32[]{:S(2)}) %collective-permute-start.14) | collective-permute-done | bytes 4128 | tf_op jit(solution)/shard_map/ppermute | solution.py:381
  53.5 1.4 %collective-permute-done.18.refs_2_ = f32[1,1,2048]{2,1,0:T(1,128)S(1)} collective-permute-done((f32[1,1,2048]{2,1,0:T(1,128)S(1)}, f32[1,1,2048]{2,1,0:T(1,128)S(1)}, u32[]{:S(2)}, u32[]{:S(2)}) %collective-permute-start.18) | collective-permute-done | bytes 8224 | tf_op jit(solution)/shard_map/ppermute | solution.py:381
  54.9 2.0 %collective-permute-done.17.refs_1_ = f32[1,1,2048]{2,1,0:T(1,128)S(1)} collective-permute-done((f32[1,1,2048]{2,1,0:T(1,128)S(1)}, f32[1,1,2048]{2,1,0:T(1,128)S(1)}, u32[]{:S(2)}, u32[]{:S(2)}) %collective-permute-start.17) | collective-permute-done | bytes 8224 | tf_op jit(solution)/shard_map/ppermute | solution.py:381
  63.7 2.3 %collective-permute-done.21.refs_1_ = f32[1,1,1024]{2,1,0:T(1,128)S(1)} collective-permute-done((f32[1,1,1024]{2,1,0:T(1,128)S(1)}, f32[1,1,1024]{2,1,0:T(1,128)S(1)}, u32[]{:S(2)}, u32[]{:S(2)}) %collective-permute-start.21) | collective-permute-done | bytes 4128 | tf_op jit(solution)/shard_map/ppermute | solution.py:381
  65.9 3.8 %shard_map.84 = (f32[1,1024]{1,0:T(1,128)S(1)}, f32[1,1,2048]{2,1,0:T(1,128)S(1)}) custom-call(f32[1024,2048]{1,0:T(8,128)S(1)} %get-tuple-element.46.s_ref, f32[1024,2048]{1,0:T(8,128)S(1)} %get-tuple-element.49.p_ref, f32[1,1024]{1,0:T(1,128)S(1)} %get-tuple-element.47.mass_ref, f32[1,1024]{1,0:T(1,128)S(1)} %get-tuple-element.50.f_ref, ...), custom_call_target="tpu_custom_call" | custom-call | tf_op jit(solution)/shard_map/pallas_call | solution.py:366
  71.9 1.6 %collective-permute-done.26.refs_3_ = f32[1,1,2048]{2,1,0:T(1,128)S(1)} collective-permute-done((f32[1,1,2048]{2,1,0:T(1,128)S(1)}, f32[1,1,2048]{2,1,0:T(1,128)S(1)}, u32[]{:S(2)}, u32[]{:S(2)}) %collective-permute-start.26) | collective-permute-done | bytes 8224 | tf_op jit(solution)/shard_map/ppermute | solution.py:381
  73.5 2.2 %collective-permute-done.25.refs_2_ = f32[1,1,2048]{2,1,0:T(1,128)S(1)} collective-permute-done((f32[1,1,2048]{2,1,0:T(1,128)S(1)}, f32[1,1,2048]{2,1,0:T(1,128)S(1)}, u32[]{:S(2)}, u32[]{:S(2)}) %collective-permute-start.25) | collective-permute-done | bytes 8224 | tf_op jit(solution)/shard_map/ppermute | solution.py:381
  78.0 5.8 %shard_map.86 = (f32[1,1024]{1,0:T(1,128)}, f32[1,2048]{1,0:T(1,128)}, f32[136,128]{1,0:T(8,128)S(1)}, f32[136,128]{1,0:T(8,128)S(1)}, f32[136,128]{1,0:T(8,128)S(1)}, /*index=5*/f32[136,128]{1,0:T(8,128)S(1)}) custom-call(s32[1]{0:T(128)} %bitcast.me_ref, f32[1024,2048]{1,0:T(8,128)S(1)} %get-tuple-element.46.s_ref, ...), custom_call_target="tpu_custom_call" | custom-call | tf_op jit(solution)/shard_map/pallas_call | solution.py:366
  84.8 2.3 %collective-permute-start.30 = (f32[136,128]{1,0:T(8,128)S(1)}, f32[136,128]{1,0:T(8,128)S(1)}, u32[]{:S(2)}, u32[]{:S(2)}) collective-permute-start(f32[136,128]{1,0:T(8,128)S(1)} %get-tuple-element.66), channel_id=1, source_target_pairs={{0,3},{1,0},{2,1},{3,2},{4,7},{5,4},{6,5},{7,6},{8,11},{9,8},{10,9... | collective-permute-start | bytes 208904 | tf_op jit(solution)/shard_map/ppermute | solution.py:381
  87.1 2.7 %collective-permute-done.28.refs_1_ = f32[136,128]{1,0:T(8,128)S(1)} collective-permute-done((f32[136,128]{1,0:T(8,128)S(1)}, f32[136,128]{1,0:T(8,128)S(1)}, u32[]{:S(2)}, u32[]{:S(2)}) %collective-permute-start.28) | collective-permute-done | bytes 69664 | tf_op jit(solution)/shard_map/ppermute | solution.py:381
  (59 shorter events, 31.3 us)
Async XLA Ops:
  0.6 7.9 %collective-permute-start = (f32[16,1024]{1,0:T(8,128)}, f32[16,1024]{1,0:T(8,128)S(1)}, u32[]{:S(2)}, u32[]{:S(2)}) collective-permute-start(f32[16,1024]{1,0:T(8,128)} %x_ref), channel_id=1, source_target_pairs={{0,3},{1,0},{2,1},{3,2},{4,7},{5,4},{6,5},{7,6},{8,11},{9,8},{10,9... | collective-permute-start | bytes 196616 | tf_op jit(solution)/shard_map/ppermute | solution.py:381
  4.6 7.5 %collective-permute-start.2 = (f32[8,2048]{1,0:T(8,128)}, f32[8,2048]{1,0:T(8,128)S(1)}, u32[]{:S(2)}, u32[]{:S(2)}) collective-permute-start(f32[8,2048]{1,0:T(8,128)} %param.6), channel_id=1, source_target_pairs={{0,16},{4,20},{8,24},{12,28},{16,0},{20,4},{24,8},{28,12},{1,17},{... | collective-permute-start | bytes 196616 | tf_op jit(solution)/shard_map/ppermute | solution.py:385
  7.2 6.4 %collective-permute-start.3 = (f32[8,2048]{1,0:T(8,128)}, f32[8,2048]{1,0:T(8,128)S(1)}, u32[]{:S(2)}, u32[]{:S(2)}) collective-permute-start(f32[8,2048]{1,0:T(8,128)} %param.6), channel_id=1, source_target_pairs={{0,24},{4,28},{8,16},{12,20},{16,8},{20,12},{24,0},{28,4},{1,25},{... | collective-permute-start | bytes 196616 | tf_op jit(solution)/shard_map/ppermute | solution.py:385
  8.5 5.2 %collective-permute-start.1 = (f32[8,2048]{1,0:T(8,128)}, f32[8,2048]{1,0:T(8,128)S(1)}, u32[]{:S(2)}, u32[]{:S(2)}) collective-permute-start(f32[8,2048]{1,0:T(8,128)} %param.6), channel_id=1, source_target_pairs={{0,8},{4,12},{8,0},{12,4},{16,24},{20,28},{24,16},{28,20},{1,9},{5... | collective-permute-start | bytes 196616 | tf_op jit(solution)/shard_map/ppermute | solution.py:385
  8.8 5.8 %collective-permute-start.4 = (f32[16,1024]{1,0:T(8,128)}, f32[16,1024]{1,0:T(8,128)S(1)}, u32[]{:S(2)}, u32[]{:S(2)}) collective-permute-start(f32[16,1024]{1,0:T(8,128)} %x_ref), channel_id=1, source_target_pairs={{0,1},{1,2},{2,3},{3,0},{4,5},{5,6},{6,7},{7,4},{8,9},{9,10},{10,1... | collective-permute-start | bytes 196616 | tf_op jit(solution)/shard_map/ppermute | solution.py:381
  10.6 4.5 %collective-permute-start.5 = (f32[16,1024]{1,0:T(8,128)}, f32[16,1024]{1,0:T(8,128)S(1)}, u32[]{:S(2)}, u32[]{:S(2)}) collective-permute-start(f32[16,1024]{1,0:T(8,128)} %x_ref), channel_id=1, source_target_pairs={{0,2},{1,3},{2,0},{3,1},{4,6},{5,7},{6,4},{7,5},{8,10},{9,11},{10,... | collective-permute-start | bytes 196616 | tf_op jit(solution)/shard_map/ppermute | solution.py:381
  21.7 3.6 %collective-permute-start.9 = (f32[1,1,1024]{2,1,0:T(1,128)S(1)}, f32[1,1,1024]{2,1,0:T(1,128)S(1)}, u32[]{:S(2)}, u32[]{:S(2)}) collective-permute-start(f32[1,1,1024]{2,1,0:T(1,128)S(1)} %get-tuple-element.48.refs_0_), channel_id=1, source_target_pairs={{0,3},{1,0},{2,1},{3,2},{4,7},{5,4},{6,5},{7,6},{8,11},{9,8},{10,9... | collective-permute-start | bytes 12296 | tf_op jit(solution)/shard_map/ppermute | solution.py:381
  23.8 4.5 %collective-permute-start.7 = (f32[1,1,1024]{2,1,0:T(1,128)S(1)}, f32[1,1,1024]{2,1,0:T(1,128)S(1)}, u32[]{:S(2)}, u32[]{:S(2)}) collective-permute-start(f32[1,1,1024]{2,1,0:T(1,128)S(1)} %get-tuple-element.48.refs_0_), channel_id=1, source_target_pairs={{0,1},{1,2},{2,3},{3,0},{4,5},{5,6},{6,7},{7,4},{8,9},{9,10},{10,1... | collective-permute-start | bytes 12296 | tf_op jit(solution)/shard_map/ppermute | solution.py:381
  31.3 4.7 %collective-permute-start.12 = (f32[1,1,2048]{2,1,0:T(1,128)S(1)}, f32[1,1,2048]{2,1,0:T(1,128)S(1)}, u32[]{:S(2)}, u32[]{:S(2)}) collective-permute-start(f32[1,1,2048]{2,1,0:T(1,128)S(1)} %get-tuple-element.52.refs_0_), channel_id=1, source_target_pairs={{0,24},{4,28},{8,0},{12,4},{16,8},{20,12},{24,16},{28,20},{1,25},{... | collective-permute-start | bytes 24584 | tf_op jit(solution)/shard_map/ppermute | solution.py:381
  33.8 4.5 %collective-permute-start.11 = (f32[1,1,2048]{2,1,0:T(1,128)S(1)}, f32[1,1,2048]{2,1,0:T(1,128)S(1)}, u32[]{:S(2)}, u32[]{:S(2)}) collective-permute-start(f32[1,1,2048]{2,1,0:T(1,128)S(1)} %get-tuple-element.52.refs_0_), channel_id=1, source_target_pairs={{0,16},{4,20},{8,24},{12,28},{16,0},{20,4},{24,8},{28,12},{1,17},{... | collective-permute-start | bytes 24584 | tf_op jit(solution)/shard_map/ppermute | solution.py:381
  34.1 5.4 %collective-permute-start.10 = (f32[1,1,2048]{2,1,0:T(1,128)S(1)}, f32[1,1,2048]{2,1,0:T(1,128)S(1)}, u32[]{:S(2)}, u32[]{:S(2)}) collective-permute-start(f32[1,1,2048]{2,1,0:T(1,128)S(1)} %get-tuple-element.52.refs_0_), channel_id=1, source_target_pairs={{0,8},{4,12},{8,16},{12,20},{16,24},{20,28},{24,0},{28,4},{1,9},{5... | collective-permute-start | bytes 24584 | tf_op jit(solution)/shard_map/ppermute | solution.py:381
  42.1 3.7 %collective-permute-start.16 = (f32[1,1,1024]{2,1,0:T(1,128)S(1)}, f32[1,1,1024]{2,1,0:T(1,128)S(1)}, u32[]{:S(2)}, u32[]{:S(2)}) collective-permute-start(f32[1,1,1024]{2,1,0:T(1,128)S(1)} %get-tuple-element.55.refs_0_), channel_id=1, source_target_pairs={{0,3},{1,0},{2,1},{3,2},{4,7},{5,4},{6,5},{7,6},{8,11},{9,8},{10,9... | collective-permute-start | bytes 12296 | tf_op jit(solution)/shard_map/ppermute | solution.py:381
  44.1 4.5 %collective-permute-start.14 = (f32[1,1,1024]{2,1,0:T(1,128)S(1)}, f32[1,1,1024]{2,1,0:T(1,128)S(1)}, u32[]{:S(2)}, u32[]{:S(2)}) collective-permute-start(f32[1,1,1024]{2,1,0:T(1,128)S(1)} %get-tuple-element.55.refs_0_), channel_id=1, source_target_pairs={{0,1},{1,2},{2,3},{3,0},{4,5},{5,6},{6,7},{7,4},{8,9},{9,10},{10,1... | collective-permute-start | bytes 12296 | tf_op jit(solution)/shard_map/ppermute | solution.py:381
  49.8 3.7 %collective-permute-start.19 = (f32[1,1,2048]{2,1,0:T(1,128)S(1)}, f32[1,1,2048]{2,1,0:T(1,128)S(1)}, u32[]{:S(2)}, u32[]{:S(2)}) collective-permute-start(f32[1,1,2048]{2,1,0:T(1,128)S(1)} %shard_map.81.refs_0_), channel_id=1, source_target_pairs={{0,24},{4,28},{8,0},{12,4},{16,8},{20,12},{24,16},{28,20},{1,25},{... | collective-permute-start | bytes 24584 | tf_op jit(solution)/shard_map/ppermute | solution.py:381
  50.3 4.5 %collective-permute-start.18 = (f32[1,1,2048]{2,1,0:T(1,128)S(1)}, f32[1,1,2048]{2,1,0:T(1,128)S(1)}, u32[]{:S(2)}, u32[]{:S(2)}) collective-permute-start(f32[1,1,2048]{2,1,0:T(1,128)S(1)} %shard_map.81.refs_0_), channel_id=1, source_target_pairs={{0,16},{4,20},{8,24},{12,28},{16,0},{20,4},{24,8},{28,12},{1,17},{... | collective-permute-start | bytes 24584 | tf_op jit(solution)/shard_map/ppermute | solution.py:381
  51.5 5.4 %collective-permute-start.17 = (f32[1,1,2048]{2,1,0:T(1,128)S(1)}, f32[1,1,2048]{2,1,0:T(1,128)S(1)}, u32[]{:S(2)}, u32[]{:S(2)}) collective-permute-start(f32[1,1,2048]{2,1,0:T(1,128)S(1)} %shard_map.81.refs_0_), channel_id=1, source_target_pairs={{0,8},{4,12},{8,16},{12,20},{16,24},{20,28},{24,0},{28,4},{1,9},{5... | collective-permute-start | bytes 24584 | tf_op jit(solution)/shard_map/ppermute | solution.py:381
  59.5 3.7 %collective-permute-start.23 = (f32[1,1,1024]{2,1,0:T(1,128)S(1)}, f32[1,1,1024]{2,1,0:T(1,128)S(1)}, u32[]{:S(2)}, u32[]{:S(2)}) collective-permute-start(f32[1,1,1024]{2,1,0:T(1,128)S(1)} %shard_map.83.refs_0_), channel_id=1, source_target_pairs={{0,3},{1,0},{2,1},{3,2},{4,7},{5,4},{6,5},{7,6},{8,11},{9,8},{10,9... | collective-permute-start | bytes 12296 | tf_op jit(solution)/shard_map/ppermute | solution.py:381
  61.4 4.5 %collective-permute-start.21 = (f32[1,1,1024]{2,1,0:T(1,128)S(1)}, f32[1,1,1024]{2,1,0:T(1,128)S(1)}, u32[]{:S(2)}, u32[]{:S(2)}) collective-permute-start(f32[1,1,1024]{2,1,0:T(1,128)S(1)} %shard_map.83.refs_0_), channel_id=1, source_target_pairs={{0,1},{1,2},{2,3},{3,0},{4,5},{5,6},{6,7},{7,4},{8,9},{9,10},{10,1... | collective-permute-start | bytes 12296 | tf_op jit(solution)/shard_map/ppermute | solution.py:381
  69.8 3.7 %collective-permute-start.26 = (f32[1,1,2048]{2,1,0:T(1,128)S(1)}, f32[1,1,2048]{2,1,0:T(1,128)S(1)}, u32[]{:S(2)}, u32[]{:S(2)}) collective-permute-start(f32[1,1,2048]{2,1,0:T(1,128)S(1)} %get-tuple-element.60.refs_0_), channel_id=1, source_target_pairs={{0,24},{4,28},{8,0},{12,4},{16,8},{20,12},{24,16},{28,20},{1,25},{... | collective-permute-start | bytes 24584 | tf_op jit(solution)/shard_map/ppermute | solution.py:381
  71.1 4.5 %collective-permute-start.25 = (f32[1,1,2048]{2,1,0:T(1,128)S(1)}, f32[1,1,2048]{2,1,0:T(1,128)S(1)}, u32[]{:S(2)}, u32[]{:S(2)}) collective-permute-start(f32[1,1,2048]{2,1,0:T(1,128)S(1)} %get-tuple-element.60.refs_0_), channel_id=1, source_target_pairs={{0,16},{4,20},{8,24},{12,28},{16,0},{20,4},{24,8},{28,12},{1,17},{... | collective-permute-start | bytes 24584 | tf_op jit(solution)/shard_map/ppermute | solution.py:381
  71.3 5.4 %collective-permute-start.24 = (f32[1,1,2048]{2,1,0:T(1,128)S(1)}, f32[1,1,2048]{2,1,0:T(1,128)S(1)}, u32[]{:S(2)}, u32[]{:S(2)}) collective-permute-start(f32[1,1,2048]{2,1,0:T(1,128)S(1)} %get-tuple-element.60.refs_0_), channel_id=1, source_target_pairs={{0,8},{4,12},{8,16},{12,20},{16,24},{20,28},{24,0},{28,4},{1,9},{5... | collective-permute-start | bytes 24584 | tf_op jit(solution)/shard_map/ppermute | solution.py:381
  83.9 6.0 %collective-permute-start.28 = (f32[136,128]{1,0:T(8,128)S(1)}, f32[136,128]{1,0:T(8,128)S(1)}, u32[]{:S(2)}, u32[]{:S(2)}) collective-permute-start(f32[136,128]{1,0:T(8,128)S(1)} %get-tuple-element.64), channel_id=1, source_target_pairs={{0,1},{1,2},{2,3},{3,0},{4,5},{5,6},{6,7},{7,4},{8,9},{9,10},{10,1... | collective-permute-start | bytes 208904 | tf_op jit(solution)/shard_map/ppermute | solution.py:381
  83.9 5.9 %collective-permute-start.29 = (f32[136,128]{1,0:T(8,128)S(1)}, f32[136,128]{1,0:T(8,128)S(1)}, u32[]{:S(2)}, u32[]{:S(2)}) collective-permute-start(f32[136,128]{1,0:T(8,128)S(1)} %get-tuple-element.65), channel_id=1, source_target_pairs={{0,2},{1,3},{2,0},{3,1},{4,6},{5,7},{6,4},{7,5},{8,10},{9,11},{10,... | collective-permute-start | bytes 208904 | tf_op jit(solution)/shard_map/ppermute | solution.py:381
  84.8 5.0 %collective-permute-start.30 = (f32[136,128]{1,0:T(8,128)S(1)}, f32[136,128]{1,0:T(8,128)S(1)}, u32[]{:S(2)}, u32[]{:S(2)}) collective-permute-start(f32[136,128]{1,0:T(8,128)S(1)} %get-tuple-element.66), channel_id=1, source_target_pairs={{0,3},{1,0},{2,1},{3,2},{4,7},{5,4},{6,5},{7,6},{8,11},{9,8},{10,9... | collective-permute-start | bytes 208904 | tf_op jit(solution)/shard_map/ppermute | solution.py:381
  (11 other events, 59.2 us)

commit v2 on v1

--- a/solution.py
+++ b/solution.py
@@ -71,9 +71,8 @@
     return pl.ds(c * LANES, LANES)
 
 
-def lanes_log_sum(s_ref, rows, pot8, top_ref, sum_ref):
-    cols = s_ref.shape[1] // LANES
-    z = [s_ref[rows, chunk(c)] + pot8[:, c * LANES : (c + 1) * LANES] for c in range(cols)]
+def lanes_log_sum(s, rows, pot8, top_ref, sum_ref):
+    z = [v + pot8[:, c * LANES : (c + 1) * LANES] for c, v in enumerate(s)]
     top = tree(jnp.maximum, z)
     top_ref[rows, :] = top
     sum_ref[rows, :] = tree(jnp.add, [jnp.exp2(v - top) for v in z])
@@ -97,7 +96,8 @@
     pot8 = jnp.broadcast_to(pot, (8, width))
 
     def strip(k, _):
-        lanes_log_sum(s_ref, eight(k), pot8, top_ref, sum_ref)
+        rows = eight(k)
+        lanes_log_sum([s_ref[rows, chunk(c)] for c in range(width // LANES)], rows, pot8, top_ref, sum_ref)
         return 0
 
     lax.fori_loop(0, n // 8, strip, 0, unroll=4)
@@ -139,10 +139,19 @@
     refs[-1][0] = whole_log_sum(refs[:-1])
 
 
-def early_kernel(mass_ref, pot_ref, x_ref, ls_ref, to_ref, xo_ref):
-    ls_ref[...] = jnp.log2(mass_ref[...])
-    to_ref[...] = pot_ref[...]
-    xo_ref[...] = x_ref[...]
+def early_kernel(*refs):
+    for ref, out_ref in zip(refs[:3], refs[3:]):
+        out_ref[...] = ref[...]
+
+
+def log_kernel(mass_ref, out_ref):
+    out_ref[...] = jnp.log2(mass_ref[...])
+
+
+def stack_kernel(*refs):
+    own = refs[0].shape[0]
+    for b, ref in enumerate(refs[:-1]):
+        refs[-1][pl.ds(b * own, own), :] = ref[...]
 
 
 def first_kernel(peers, xplan, yplan, me_ref, pot_ref, *refs):
@@ -158,7 +167,7 @@
         xs[pl.ds(pl.multiple_of(lax.rem(me_tgt - d + peers, peers) * own, 8), own), :] = part[...]
     x = xs[...]
     xn_ref[...] = jnp.sum(x * x, axis=0, keepdims=True) / x.shape[0]
-    x1, x2, x3 = pieces(x)
+    x1, x2, _ = pieces(x)
     for part, owners in zip(yparts, yplan):
         if owners is None:
             yo_ref[...] = part[...]
@@ -170,8 +179,8 @@
     yn = jnp.sum(y * y, axis=0, keepdims=True) / y.shape[0]
     yn_ref[...] = yn
     k = y.shape[0]
-    y1, y2, y3 = pieces(y * (2.0 / (k * UNIT)))
-    for p, (xp, yp) in enumerate(((x1, y1), (x1, y2), (x2, y1), (x2, y2), (x1, y3), (x3, y1))):
+    y1, y2, _ = pieces(y * (2.0 / (k * UNIT)))
+    for p, (xp, yp) in enumerate(((x1, y1), (x1, y2), (x2, y1), (x2, y2))):
         xw[pl.ds(p * k, k), :] = xp
         yw[pl.ds(p * k, k), :] = yp
     n, width = s_ref.shape
@@ -179,12 +188,14 @@
     step = 256
     for b in range(n // step + 1):
         if b < n // step:
-            s_ref[pl.ds(b * step, step), :] = lax.dot_general(
-                xw[:, pl.ds(b * step, step)], yw[...], (((0,), (0,)), ((), ())), preferred_element_type=F32
+            rows = pl.ds(b * step, step)
+            s_ref[rows, :] = lax.dot_general(
+                xw[:, rows], yw[...], (((0,), (0,)), ((), ())), preferred_element_type=F32
             )
         if b > 0:
             for r in range((b - 1) * step, b * step, 8):
-                lanes_log_sum(s_ref, pl.ds(r, 8), pot8, top_ref, sum_ref)
+                rows = pl.ds(r, 8)
+                lanes_log_sum([s_ref[rows, chunk(c)] for c in range(width // LANES)], rows, pot8, top_ref, sum_ref)
     l_ref[0] = join_lanes(top_ref, sum_ref)
 
 
@@ -315,15 +326,16 @@
         yw[pl.ds(k, LANES - k), :] = jnp.where(at == 0, s1, jnp.where(at == 1, s2, 0.0)).astype(BF16)
         yw[pl.ds(LANES, k), :] = y2
         yw[pl.ds(LANES + k, LANES - k), :] = jnp.zeros((LANES - k, width), BF16)
+        dims = (((1,), (1,)), ((), ()))
         for b in range(n // step):
-            w = weight(pl.ds(b * step, step))
+            rows = pl.ds(b * step, step)
+            w = weight(rows)
             w1 = w.astype(BF16)
             w2 = (w - w1.astype(F32)).astype(BF16)
-            dims = (((1,), (1,)), ((), ()))
             out = lax.dot_general(w1, yw[...], dims, preferred_element_type=F32) + lax.dot_general(
                 w2, yw[...], dims, preferred_element_type=F32
             )
-            acc[pl.ds(b * step, step), :] = out[:, :LANES] + out[:, LANES:]
+            acc[rows, :] = out[:, :LANES] + out[:, LANES:]
         total = acc[...].T * rescale
         den = total[k : k + 1, :] + total[k + 1 : k + 2, :]
         for t in range(peers):
@@ -362,13 +374,14 @@
         out_ref[:, chunk(c)] = num / den
 
 
-def call(kernel, outs, scratch, ins, out_specs=None):
+def call(kernel, outs, scratch, ins, out_specs=None, cost=None):
     return pl.pallas_call(
         kernel,
         out_shape=[o if isinstance(o, jax.ShapeDtypeStruct) else jax.ShapeDtypeStruct(o, F32) for o in outs],
         in_specs=[spec for spec, _ in ins],
         out_specs=out_specs or [VMEM] * len(outs),
         scratch_shapes=scratch,
+        cost_estimate=cost,
         compiler_params=pltpu.CompilerParams(vmem_limit_bytes=20 * 2**20),
     )(*[a for _, a in ins])
 
@@ -405,14 +418,14 @@
     return [v] + [turn(v, "tgt", size, d) for d in range(1, size)], list(range(size))
 
 
-def gather_tgt(v, size, other):
+def gather_tgt(v, own, size, other):
     if v.shape[0] % 8 or size & (size - 1):
         return [lax.all_gather(v, "src", axis=0, tiled=True)], [None], other
     order = list(range(0, size, 2))
     far = [flip(v, "src", size, d) for d in order[2:]]
     again, last = lax.optimization_barrier((v, other[-1]))
     near = [flip(again, "src", size, d) for d in order[1:2]]
-    mine = jnp.concatenate([v] + near + far, axis=0)
+    (mine,) = call(stack_kernel, [(len(order) * v.shape[0], v.shape[1])], [], put(own, *near, *far))
     mine, *other = lax.optimization_barrier([mine] + other[:-1] + [last])
     return [mine, flip(mine, "src", size, 1)], [order, [d + 1 for d in order]], other
 
@@ -427,16 +440,28 @@
     lane = pltpu.VMEM((n, LANES), F32)
     me = lax.axis_index(("src", "tgt")).astype(jnp.int32).reshape(1)
     xs, xplan = gather_src(src_pts, peers_tgt)
-    sm, pot = src_mass.reshape(row), init_pot.reshape(col)
-    ys, yplan, (sm, pot, *xs) = gather_tgt(tgt_pts, peers_src, [sm, pot] + xs)
-    tm = tgt_mass.reshape(col)
-    sm, pot, x = call(early_kernel, [row, col, xs[0].shape], [], put(sm, pot, xs[0]))
+    pot, x, y = call(
+        early_kernel, [col, src_pts.shape, tgt_pts.shape], [], put(init_pot.reshape(col), src_pts, tgt_pts)
+    )
+    if xplan[0] is not None:
+        xs[0] = x
+    ys, yplan, xs = gather_tgt(tgt_pts, y, peers_src, xs)
+    sm, tm = src_mass.reshape(row), tgt_mass.reshape(col)
     s, l, xn, yn, yo = call(
         functools.partial(first_kernel, peers_tgt, xplan, yplan),
         [(n, width), rows, row, col, (k, width)],
-        [pltpu.VMEM((k, n), F32), pltpu.VMEM((6 * k, n), BF16), pltpu.VMEM((6 * k, width), BF16), lane, lane],
-        [(SMEM, me)] + put(pot, x, *xs[1:], *ys),
+        [
+            pltpu.VMEM((k, n), F32),
+            pltpu.VMEM((4 * k, n), BF16),
+            pltpu.VMEM((4 * k, width), BF16),
+            lane,
+            lane,
+        ],
+        [(SMEM, me)] + put(pot, *xs, *ys),
+        cost=pl.CostEstimate(flops=8 * k * n * width, transcendentals=n * width, bytes_accessed=8 * n * width),
     )
+    sm, l = lax.optimization_barrier((sm, l))
+    (sm,) = call(log_kernel, [row], [], put(sm), cost=pl.CostEstimate(flops=n, transcendentals=n, bytes_accessed=8 * n))
     parts = join_rows(l, "tgt", peers_tgt)
     f, p, top, l = call(
         functools.partial(src_first_kernel, len(parts)), [row, (n, width), col, cols], [lane], put(s, sm, *parts)

time: 90.8 us -> 89.7 us (0.988)
    unnamed x8 -> x10, local copies, waits for them, and re-layouts: 2.23 us -> 3.06 us
    pallas_call x12 -> x14, Pallas kernels: 21.5 us -> 20.8 us  [call(): pl.pallas_call(kernel, out_shape=[o if isinstance(o, jax.ShapeDtypeStruct...]
  transfers between devices with their start and end apart: 31 -> 31, of which waited for: 23 -> 24; matrix products, arithmetic and copies ran while one was open for 1% -> 0% of each run, Pallas kernels for 0% -> 0%
where the time goes in v2:
time: 89.7 us; the launch traced here: 89.4 us
  starting transfers between devices  34.9 us (39%)
  waiting for transfers between devices  29.9 us (33%)
  Pallas kernels  20.8 us (23%)
  local copies, waits for them, and re-layouts  3.06 us (3%)
    ppermute x24, starting transfers between devices, turn(): return lax.ppermute(v, axis, [(i, (i + d) % size) for i in range(size)])  30.3 us
    ppermute x24, waiting for transfers between devices, turn(): return lax.ppermute(v, axis, [(i, (i + d) % size) for i in range(size)])  24.8 us
    pallas_call x14, Pallas kernels, call(): pl.pallas_call(kernel, out_shape=[o if isinstance(o, jax.ShapeDtypeStruct...  20.8 us
    ppermute x7, waiting for transfers between devices, flip(): return lax.ppermute(v, axis, [(i, i ^ bit) for i in range(size)])  5.02 us
    ppermute x7, starting transfers between devices, flip(): return lax.ppermute(v, axis, [(i, i ^ bit) for i in range(size)])  4.6 us
    unnamed x10, local copies, waits for them, and re-layouts  3.06 us
  transfers between devices with their start and end apart: 31, of which 24 were waited for; matrix products, arithmetic and copies ran while one was open for 0% of the time, Pallas kernels for 0%

profile of v2, /device:TPU:0, one launch (start us, length us, event | category | flops | bytes accessed | tf_op | source)
XLA Modules:
  0.0 89.4 jit_solution(812237117527280311)
XLA Ops:
  0.6 3.9 %collective-permute-start = (f32[16,1024]{1,0:T(8,128)}, f32[16,1024]{1,0:T(8,128)S(1)}, u32[]{:S(2)}, u32[]{:S(2)}) collective-permute-start(f32[16,1024]{1,0:T(8,128)} %refs_1_.1), channel_id=1, source_target_pairs={{0,3},{1,0},{2,1},{3,2},{4,7},{5,4},{6,5},{7,6},{8,11},{9,8},{10,9... | collective-permute-start | bytes 196616 | tf_op jit(solution)/shard_map/ppermute | solution.py:394
  4.6 3.6 %collective-permute-start.3 = (f32[8,2048]{1,0:T(8,128)}, f32[8,2048]{1,0:T(8,128)S(1)}, u32[]{:S(2)}, u32[]{:S(2)}) collective-permute-start(f32[8,2048]{1,0:T(8,128)} %refs_2_.1), channel_id=1, source_target_pairs={{0,24},{4,28},{8,16},{12,20},{16,8},{20,12},{24,0},{28,4},{1,25},{... | collective-permute-start | bytes 196616 | tf_op jit(solution)/shard_map/ppermute | solution.py:398
  9.7 2.4 %collective-permute-start.4 = (f32[16,1024]{1,0:T(8,128)}, f32[16,1024]{1,0:T(8,128)S(1)}, u32[]{:S(2)}, u32[]{:S(2)}) collective-permute-start(f32[16,1024]{1,0:T(8,128)} %refs_1_.1), channel_id=1, source_target_pairs={{0,1},{1,2},{2,3},{3,0},{4,5},{5,6},{6,7},{7,4},{8,9},{9,10},{10,1... | collective-permute-start | bytes 196616 | tf_op jit(solution)/shard_map/ppermute | solution.py:394
  15.1 1.5 %collective-permute-done.6.refs_5_ = f32[32,2048]{1,0:T(8,128)S(1)} collective-permute-done((f32[32,2048]{1,0:T(8,128)S(1)}, f32[32,2048]{1,0:T(8,128)S(1)}, u32[]{:S(2)}, u32[]{:S(2)}) %collective-permute-start.6) | collective-permute-done | bytes 262176 | tf_op jit(solution)/shard_map/ppermute | solution.py:398
  16.6 3.7 %shard_map.78 = (f32[1024,2048]{1,0:T(8,128)S(1)}, f32[1,1,1024]{2,1,0:T(1,128)S(1)}, f32[1,1024]{1,0:T(1,128)S(1)}, f32[1,2048]{1,0:T(1,128)S(1)}, f32[64,2048]{1,0:T(8,128)S(1)}) custom-call(s32[1]{0:T(128)} %bitcast.me_ref, f32[1,2048]{1,0:T(1,128)S(1)} %get-tuple-element.35.pot_ref, f32[16,1024]{1,0:T(8,128)S(1)} %get-tuple-element.40.refs_0_, ...), custom_call_target="tpu_custom_call" | custom-call | flops 1073741824 | bytes 16777216 | tf_op jit(solution)/shard_map/pallas_call | solution.py:378
  20.3 1.5 %collective-permute-start.9 = (f32[1,1,1024]{2,1,0:T(1,128)S(1)}, f32[1,1,1024]{2,1,0:T(1,128)S(1)}, u32[]{:S(2)}, u32[]{:S(2)}) collective-permute-start(f32[1,1,1024]{2,1,0:T(1,128)S(1)} %get-tuple-element.48.refs_0_), channel_id=1, source_target_pairs={{0,3},{1,0},{2,1},{3,2},{4,7},{5,4},{6,5},{7,6},{8,11},{9,8},{10,9... | collective-permute-start | bytes 12296 | tf_op jit(solution)/shard_map/ppermute | solution.py:394
  21.8 1.5 %collective-permute-start.8 = (f32[1,1,1024]{2,1,0:T(1,128)S(1)}, f32[1,1,1024]{2,1,0:T(1,128)S(1)}, u32[]{:S(2)}, u32[]{:S(2)}) collective-permute-start(f32[1,1,1024]{2,1,0:T(1,128)S(1)} %get-tuple-element.48.refs_0_), channel_id=1, source_target_pairs={{0,2},{1,3},{2,0},{3,1},{4,6},{5,7},{6,4},{7,5},{8,10},{9,11},{10,... | collective-permute-start | bytes 12296 | tf_op jit(solution)/shard_map/ppermute | solution.py:394
  25.4 2.4 %collective-permute-done.7.refs_1_ = f32[1,1,1024]{2,1,0:T(1,128)S(1)} collective-permute-done((f32[1,1,1024]{2,1,0:T(1,128)S(1)}, f32[1,1,1024]{2,1,0:T(1,128)S(1)}, u32[]{:S(2)}, u32[]{:S(2)}) %collective-permute-start.7) | collective-permute-done | bytes 4128 | tf_op jit(solution)/shard_map/ppermute | solution.py:394
  27.8 2.9 %shard_map.80 = (f32[1,1024]{1,0:T(1,128)S(1)}, f32[1024,2048]{1,0:T(8,128)S(1)}, f32[1,2048]{1,0:T(1,128)S(1)}, f32[1,1,2048]{2,1,0:T(1,128)S(1)}) custom-call(f32[1024,2048]{1,0:T(8,128)S(1)} %get-tuple-element.45.s_ref, f32[1,1024]{1,0:T(1,128)S(1)} %shard_map.79.mass_ref, f32[1,1,1024]{2,1,0:T(1,128)S(1)} %get-tuple-element.48.refs_0_, ...), custom_call_target="tpu_custom_call" | custom-call | tf_op jit(solution)/shard_map/pallas_call | solution.py:378
  30.8 2.5 %collective-permute-start.12 = (f32[1,1,2048]{2,1,0:T(1,128)S(1)}, f32[1,1,2048]{2,1,0:T(1,128)S(1)}, u32[]{:S(2)}, u32[]{:S(2)}) collective-permute-start(f32[1,1,2048]{2,1,0:T(1,128)S(1)} %get-tuple-element.52.refs_0_), channel_id=1, source_target_pairs={{0,24},{4,28},{8,0},{12,4},{16,8},{20,12},{24,16},{28,20},{1,25},{... | collective-permute-start | bytes 24584 | tf_op jit(solution)/shard_map/ppermute | solution.py:394
  33.5 1.9 %collective-permute-start.10 = (f32[1,1,2048]{2,1,0:T(1,128)S(1)}, f32[1,1,2048]{2,1,0:T(1,128)S(1)}, u32[]{:S(2)}, u32[]{:S(2)}) collective-permute-start(f32[1,1,2048]{2,1,0:T(1,128)S(1)} %get-tuple-element.52.refs_0_), channel_id=1, source_target_pairs={{0,8},{4,12},{8,16},{12,20},{16,24},{20,28},{24,0},{28,4},{1,9},{5... | collective-permute-start | bytes 24584 | tf_op jit(solution)/shard_map/ppermute | solution.py:394
  35.4 2.4 %collective-permute-done.11.refs_2_ = f32[1,1,2048]{2,1,0:T(1,128)S(1)} collective-permute-done((f32[1,1,2048]{2,1,0:T(1,128)S(1)}, f32[1,1,2048]{2,1,0:T(1,128)S(1)}, u32[]{:S(2)}, u32[]{:S(2)}) %collective-permute-start.11) | collective-permute-done | bytes 8224 | tf_op jit(solution)/shard_map/ppermute | solution.py:394
  41.9 1.5 %collective-permute-start.15 = (f32[1,1,1024]{2,1,0:T(1,128)S(1)}, f32[1,1,1024]{2,1,0:T(1,128)S(1)}, u32[]{:S(2)}, u32[]{:S(2)}) collective-permute-start(f32[1,1,1024]{2,1,0:T(1,128)S(1)} %get-tuple-element.55.refs_0_), channel_id=1, source_target_pairs={{0,2},{1,3},{2,0},{3,1},{4,6},{5,7},{6,4},{7,5},{8,10},{9,11},{10,... | collective-permute-start | bytes 12296 | tf_op jit(solution)/shard_map/ppermute | solution.py:394
  45.5 2.4 %collective-permute-done.14.refs_1_ = f32[1,1,1024]{2,1,0:T(1,128)S(1)} collective-permute-done((f32[1,1,1024]{2,1,0:T(1,128)S(1)}, f32[1,1,1024]{2,1,0:T(1,128)S(1)}, u32[]{:S(2)}, u32[]{:S(2)}) %collective-permute-start.14) | collective-permute-done | bytes 4128 | tf_op jit(solution)/shard_map/ppermute | solution.py:394
  50.4 1.9 %collective-permute-start.17 = (f32[1,1,2048]{2,1,0:T(1,128)S(1)}, f32[1,1,2048]{2,1,0:T(1,128)S(1)}, u32[]{:S(2)}, u32[]{:S(2)}) collective-permute-start(f32[1,1,2048]{2,1,0:T(1,128)S(1)} %shard_map.83.refs_0_), channel_id=1, source_target_pairs={{0,8},{4,12},{8,16},{12,20},{16,24},{20,28},{24,0},{28,4},{1,9},{5... | collective-permute-start | bytes 24584 | tf_op jit(solution)/shard_map/ppermute | solution.py:394
  52.8 1.5 %collective-permute-done.18.refs_2_ = f32[1,1,2048]{2,1,0:T(1,128)S(1)} collective-permute-done((f32[1,1,2048]{2,1,0:T(1,128)S(1)}, f32[1,1,2048]{2,1,0:T(1,128)S(1)}, u32[]{:S(2)}, u32[]{:S(2)}) %collective-permute-start.18) | collective-permute-done | bytes 8224 | tf_op jit(solution)/shard_map/ppermute | solution.py:394
  54.3 1.5 %collective-permute-done.17.refs_1_ = f32[1,1,2048]{2,1,0:T(1,128)S(1)} collective-permute-done((f32[1,1,2048]{2,1,0:T(1,128)S(1)}, f32[1,1,2048]{2,1,0:T(1,128)S(1)}, u32[]{:S(2)}, u32[]{:S(2)}) %collective-permute-start.17) | collective-permute-done | bytes 8224 | tf_op jit(solution)/shard_map/ppermute | solution.py:394
  63.2 1.4 %collective-permute-done.21.refs_1_ = f32[1,1,1024]{2,1,0:T(1,128)S(1)} collective-permute-done((f32[1,1,1024]{2,1,0:T(1,128)S(1)}, f32[1,1,1024]{2,1,0:T(1,128)S(1)}, u32[]{:S(2)}, u32[]{:S(2)}) %collective-permute-start.21) | collective-permute-done | bytes 4128 | tf_op jit(solution)/shard_map/ppermute | solution.py:394
  64.6 3.8 %shard_map.86 = (f32[1,1024]{1,0:T(1,128)S(1)}, f32[1,1,2048]{2,1,0:T(1,128)S(1)}) custom-call(f32[1024,2048]{1,0:T(8,128)S(1)} %get-tuple-element.45.s_ref, f32[1024,2048]{1,0:T(8,128)S(1)} %get-tuple-element.49.p_ref, f32[1,1024]{1,0:T(1,128)S(1)} %shard_map.79.mass_ref, f32[1,1024]{1,0:T(1,128)S(1)} %get-tuple-element.50.f_ref, ...), custom_call_target="tpu_custom_call" | custom-call | tf_op jit(solution)/shard_map/pallas_call | solution.py:378
  70.5 1.7 %collective-permute-done.26.refs_3_ = f32[1,1,2048]{2,1,0:T(1,128)S(1)} collective-permute-done((f32[1,1,2048]{2,1,0:T(1,128)S(1)}, f32[1,1,2048]{2,1,0:T(1,128)S(1)}, u32[]{:S(2)}, u32[]{:S(2)}) %collective-permute-start.26) | collective-permute-done | bytes 8224 | tf_op jit(solution)/shard_map/ppermute | solution.py:394
  72.2 1.8 %collective-permute-done.25.refs_2_ = f32[1,1,2048]{2,1,0:T(1,128)S(1)} collective-permute-done((f32[1,1,2048]{2,1,0:T(1,128)S(1)}, f32[1,1,2048]{2,1,0:T(1,128)S(1)}, u32[]{:S(2)}, u32[]{:S(2)}) %collective-permute-start.25) | collective-permute-done | bytes 8224 | tf_op jit(solution)/shard_map/ppermute | solution.py:394
  76.2 5.8 %shard_map.88 = (f32[1,1024]{1,0:T(1,128)}, f32[1,2048]{1,0:T(1,128)}, f32[136,128]{1,0:T(8,128)S(1)}, f32[136,128]{1,0:T(8,128)S(1)}, f32[136,128]{1,0:T(8,128)S(1)}, /*index=5*/f32[136,128]{1,0:T(8,128)S(1)}) custom-call(s32[1]{0:T(128)} %bitcast.me_ref, f32[1024,2048]{1,0:T(8,128)S(1)} %get-tuple-element.45.s_ref, ...), custom_call_target="tpu_custom_call" | custom-call | tf_op jit(solution)/shard_map/pallas_call | solution.py:378
  82.7 1.5 %collective-permute-start.29 = (f32[136,128]{1,0:T(8,128)S(1)}, f32[136,128]{1,0:T(8,128)S(1)}, u32[]{:S(2)}, u32[]{:S(2)}) collective-permute-start(f32[136,128]{1,0:T(8,128)S(1)} %get-tuple-element.65), channel_id=1, source_target_pairs={{0,2},{1,3},{2,0},{3,1},{4,6},{5,7},{6,4},{7,5},{8,10},{9,11},{10,... | collective-permute-start | bytes 208904 | tf_op jit(solution)/shard_map/ppermute | solution.py:394
  84.2 2.3 %collective-permute-start.30 = (f32[136,128]{1,0:T(8,128)S(1)}, f32[136,128]{1,0:T(8,128)S(1)}, u32[]{:S(2)}, u32[]{:S(2)}) collective-permute-start(f32[136,128]{1,0:T(8,128)S(1)} %get-tuple-element.66), channel_id=1, source_target_pairs={{0,3},{1,0},{2,1},{3,2},{4,7},{5,4},{6,5},{7,6},{8,11},{9,8},{10,9... | collective-permute-start | bytes 208904 | tf_op jit(solution)/shard_map/ppermute | solution.py:394
  (62 shorter events, 30.9 us)
Async XLA Ops:
  0.6 7.6 %collective-permute-start = (f32[16,1024]{1,0:T(8,128)}, f32[16,1024]{1,0:T(8,128)S(1)}, u32[]{:S(2)}, u32[]{:S(2)}) collective-permute-start(f32[16,1024]{1,0:T(8,128)} %refs_1_.1), channel_id=1, source_target_pairs={{0,3},{1,0},{2,1},{3,2},{4,7},{5,4},{6,5},{7,6},{8,11},{9,8},{10,9... | collective-permute-start | bytes 196616 | tf_op jit(solution)/shard_map/ppermute | solution.py:394
  4.6 9.9 %collective-permute-start.3 = (f32[8,2048]{1,0:T(8,128)}, f32[8,2048]{1,0:T(8,128)S(1)}, u32[]{:S(2)}, u32[]{:S(2)}) collective-permute-start(f32[8,2048]{1,0:T(8,128)} %refs_2_.1), channel_id=1, source_target_pairs={{0,24},{4,28},{8,16},{12,20},{16,8},{20,12},{24,0},{28,4},{1,25},{... | collective-permute-start | bytes 196616 | tf_op jit(solution)/shard_map/ppermute | solution.py:398
  8.2 6.3 %collective-permute-start.2 = (f32[8,2048]{1,0:T(8,128)}, f32[8,2048]{1,0:T(8,128)S(1)}, u32[]{:S(2)}, u32[]{:S(2)}) collective-permute-start(f32[8,2048]{1,0:T(8,128)} %refs_2_.1), channel_id=1, source_target_pairs={{0,16},{4,20},{8,24},{12,28},{16,0},{20,4},{24,8},{28,12},{1,17},{... | collective-permute-start | bytes 196616 | tf_op jit(solution)/shard_map/ppermute | solution.py:398
  8.2 6.3 %collective-permute-start.1 = (f32[8,2048]{1,0:T(8,128)}, f32[8,2048]{1,0:T(8,128)S(1)}, u32[]{:S(2)}, u32[]{:S(2)}) collective-permute-start(f32[8,2048]{1,0:T(8,128)} %refs_2_.1), channel_id=1, source_target_pairs={{0,8},{4,12},{8,0},{12,4},{16,24},{20,28},{24,16},{28,20},{1,9},{5... | collective-permute-start | bytes 196616 | tf_op jit(solution)/shard_map/ppermute | solution.py:398
  9.0 5.6 %collective-permute-start.5 = (f32[16,1024]{1,0:T(8,128)}, f32[16,1024]{1,0:T(8,128)S(1)}, u32[]{:S(2)}, u32[]{:S(2)}) collective-permute-start(f32[16,1024]{1,0:T(8,128)} %refs_1_.1), channel_id=1, source_target_pairs={{0,2},{1,3},{2,0},{3,1},{4,6},{5,7},{6,4},{7,5},{8,10},{9,11},{10,... | collective-permute-start | bytes 196616 | tf_op jit(solution)/shard_map/ppermute | solution.py:394
  9.7 5.4 %collective-permute-start.4 = (f32[16,1024]{1,0:T(8,128)}, f32[16,1024]{1,0:T(8,128)S(1)}, u32[]{:S(2)}, u32[]{:S(2)}) collective-permute-start(f32[16,1024]{1,0:T(8,128)} %refs_1_.1), channel_id=1, source_target_pairs={{0,1},{1,2},{2,3},{3,0},{4,5},{5,6},{6,7},{7,4},{8,9},{9,10},{10,1... | collective-permute-start | bytes 196616 | tf_op jit(solution)/shard_map/ppermute | solution.py:394
  20.3 4.1 %collective-permute-start.9 = (f32[1,1,1024]{2,1,0:T(1,128)S(1)}, f32[1,1,1024]{2,1,0:T(1,128)S(1)}, u32[]{:S(2)}, u32[]{:S(2)}) collective-permute-start(f32[1,1,1024]{2,1,0:T(1,128)S(1)} %get-tuple-element.48.refs_0_), channel_id=1, source_target_pairs={{0,3},{1,0},{2,1},{3,2},{4,7},{5,4},{6,5},{7,6},{8,11},{9,8},{10,9... | collective-permute-start | bytes 12296 | tf_op jit(solution)/shard_map/ppermute | solution.py:394
  23.3 4.5 %collective-permute-start.7 = (f32[1,1,1024]{2,1,0:T(1,128)S(1)}, f32[1,1,1024]{2,1,0:T(1,128)S(1)}, u32[]{:S(2)}, u32[]{:S(2)}) collective-permute-start(f32[1,1,1024]{2,1,0:T(1,128)S(1)} %get-tuple-element.48.refs_0_), channel_id=1, source_target_pairs={{0,1},{1,2},{2,3},{3,0},{4,5},{5,6},{6,7},{7,4},{8,9},{9,10},{10,1... | collective-permute-start | bytes 12296 | tf_op jit(solution)/shard_map/ppermute | solution.py:394
  30.8 4.7 %collective-permute-start.12 = (f32[1,1,2048]{2,1,0:T(1,128)S(1)}, f32[1,1,2048]{2,1,0:T(1,128)S(1)}, u32[]{:S(2)}, u32[]{:S(2)}) collective-permute-start(f32[1,1,2048]{2,1,0:T(1,128)S(1)} %get-tuple-element.52.refs_0_), channel_id=1, source_target_pairs={{0,24},{4,28},{8,0},{12,4},{16,8},{20,12},{24,16},{28,20},{1,25},{... | collective-permute-start | bytes 24584 | tf_op jit(solution)/shard_map/ppermute | solution.py:394
  33.3 4.5 %collective-permute-start.11 = (f32[1,1,2048]{2,1,0:T(1,128)S(1)}, f32[1,1,2048]{2,1,0:T(1,128)S(1)}, u32[]{:S(2)}, u32[]{:S(2)}) collective-permute-start(f32[1,1,2048]{2,1,0:T(1,128)S(1)} %get-tuple-element.52.refs_0_), channel_id=1, source_target_pairs={{0,16},{4,20},{8,24},{12,28},{16,0},{20,4},{24,8},{28,12},{1,17},{... | collective-permute-start | bytes 24584 | tf_op jit(solution)/shard_map/ppermute | solution.py:394
  33.5 5.4 %collective-permute-start.10 = (f32[1,1,2048]{2,1,0:T(1,128)S(1)}, f32[1,1,2048]{2,1,0:T(1,128)S(1)}, u32[]{:S(2)}, u32[]{:S(2)}) collective-permute-start(f32[1,1,2048]{2,1,0:T(1,128)S(1)} %get-tuple-element.52.refs_0_), channel_id=1, source_target_pairs={{0,8},{4,12},{8,16},{12,20},{16,24},{20,28},{24,0},{28,4},{1,9},{5... | collective-permute-start | bytes 24584 | tf_op jit(solution)/shard_map/ppermute | solution.py:394
  41.5 3.7 %collective-permute-start.16 = (f32[1,1,1024]{2,1,0:T(1,128)S(1)}, f32[1,1,1024]{2,1,0:T(1,128)S(1)}, u32[]{:S(2)}, u32[]{:S(2)}) collective-permute-start(f32[1,1,1024]{2,1,0:T(1,128)S(1)} %get-tuple-element.55.refs_0_), channel_id=1, source_target_pairs={{0,3},{1,0},{2,1},{3,2},{4,7},{5,4},{6,5},{7,6},{8,11},{9,8},{10,9... | collective-permute-start | bytes 12296 | tf_op jit(solution)/shard_map/ppermute | solution.py:394
  43.4 4.5 %collective-permute-start.14 = (f32[1,1,1024]{2,1,0:T(1,128)S(1)}, f32[1,1,1024]{2,1,0:T(1,128)S(1)}, u32[]{:S(2)}, u32[]{:S(2)}) collective-permute-start(f32[1,1,1024]{2,1,0:T(1,128)S(1)} %get-tuple-element.55.refs_0_), channel_id=1, source_target_pairs={{0,1},{1,2},{2,3},{3,0},{4,5},{5,6},{6,7},{7,4},{8,9},{9,10},{10,1... | collective-permute-start | bytes 12296 | tf_op jit(solution)/shard_map/ppermute | solution.py:394
  49.1 3.7 %collective-permute-start.19 = (f32[1,1,2048]{2,1,0:T(1,128)S(1)}, f32[1,1,2048]{2,1,0:T(1,128)S(1)}, u32[]{:S(2)}, u32[]{:S(2)}) collective-permute-start(f32[1,1,2048]{2,1,0:T(1,128)S(1)} %shard_map.83.refs_0_), channel_id=1, source_target_pairs={{0,24},{4,28},{8,0},{12,4},{16,8},{20,12},{24,16},{28,20},{1,25},{... | collective-permute-start | bytes 24584 | tf_op jit(solution)/shard_map/ppermute | solution.py:394
  49.7 4.5 %collective-permute-start.18 = (f32[1,1,2048]{2,1,0:T(1,128)S(1)}, f32[1,1,2048]{2,1,0:T(1,128)S(1)}, u32[]{:S(2)}, u32[]{:S(2)}) collective-permute-start(f32[1,1,2048]{2,1,0:T(1,128)S(1)} %shard_map.83.refs_0_), channel_id=1, source_target_pairs={{0,16},{4,20},{8,24},{12,28},{16,0},{20,4},{24,8},{28,12},{1,17},{... | collective-permute-start | bytes 24584 | tf_op jit(solution)/shard_map/ppermute | solution.py:394
  50.4 5.4 %collective-permute-start.17 = (f32[1,1,2048]{2,1,0:T(1,128)S(1)}, f32[1,1,2048]{2,1,0:T(1,128)S(1)}, u32[]{:S(2)}, u32[]{:S(2)}) collective-permute-start(f32[1,1,2048]{2,1,0:T(1,128)S(1)} %shard_map.83.refs_0_), channel_id=1, source_target_pairs={{0,8},{4,12},{8,16},{12,20},{16,24},{20,28},{24,0},{28,4},{1,9},{5... | collective-permute-start | bytes 24584 | tf_op jit(solution)/shard_map/ppermute | solution.py:394
  58.4 3.7 %collective-permute-start.23 = (f32[1,1,1024]{2,1,0:T(1,128)S(1)}, f32[1,1,1024]{2,1,0:T(1,128)S(1)}, u32[]{:S(2)}, u32[]{:S(2)}) collective-permute-start(f32[1,1,1024]{2,1,0:T(1,128)S(1)} %shard_map.85.refs_0_), channel_id=1, source_target_pairs={{0,3},{1,0},{2,1},{3,2},{4,7},{5,4},{6,5},{7,6},{8,11},{9,8},{10,9... | collective-permute-start | bytes 12296 | tf_op jit(solution)/shard_map/ppermute | solution.py:394
  60.1 4.5 %collective-permute-start.21 = (f32[1,1,1024]{2,1,0:T(1,128)S(1)}, f32[1,1,1024]{2,1,0:T(1,128)S(1)}, u32[]{:S(2)}, u32[]{:S(2)}) collective-permute-start(f32[1,1,1024]{2,1,0:T(1,128)S(1)} %shard_map.85.refs_0_), channel_id=1, source_target_pairs={{0,1},{1,2},{2,3},{3,0},{4,5},{5,6},{6,7},{7,4},{8,9},{9,10},{10,1... | collective-permute-start | bytes 12296 | tf_op jit(solution)/shard_map/ppermute | solution.py:394
  68.4 3.8 %collective-permute-start.26 = (f32[1,1,2048]{2,1,0:T(1,128)S(1)}, f32[1,1,2048]{2,1,0:T(1,128)S(1)}, u32[]{:S(2)}, u32[]{:S(2)}) collective-permute-start(f32[1,1,2048]{2,1,0:T(1,128)S(1)} %get-tuple-element.60.refs_0_), channel_id=1, source_target_pairs={{0,24},{4,28},{8,0},{12,4},{16,8},{20,12},{24,16},{28,20},{1,25},{... | collective-permute-start | bytes 24584 | tf_op jit(solution)/shard_map/ppermute | solution.py:394
  69.4 4.5 %collective-permute-start.25 = (f32[1,1,2048]{2,1,0:T(1,128)S(1)}, f32[1,1,2048]{2,1,0:T(1,128)S(1)}, u32[]{:S(2)}, u32[]{:S(2)}) collective-permute-start(f32[1,1,2048]{2,1,0:T(1,128)S(1)} %get-tuple-element.60.refs_0_), channel_id=1, source_target_pairs={{0,16},{4,20},{8,24},{12,28},{16,0},{20,4},{24,8},{28,12},{1,17},{... | collective-permute-start | bytes 24584 | tf_op jit(solution)/shard_map/ppermute | solution.py:394
  69.5 5.4 %collective-permute-start.24 = (f32[1,1,2048]{2,1,0:T(1,128)S(1)}, f32[1,1,2048]{2,1,0:T(1,128)S(1)}, u32[]{:S(2)}, u32[]{:S(2)}) collective-permute-start(f32[1,1,2048]{2,1,0:T(1,128)S(1)} %get-tuple-element.60.refs_0_), channel_id=1, source_target_pairs={{0,8},{4,12},{8,16},{12,20},{16,24},{20,28},{24,0},{28,4},{1,9},{5... | collective-permute-start | bytes 24584 | tf_op jit(solution)/shard_map/ppermute | solution.py:394
  82.0 5.6 %collective-permute-start.28 = (f32[136,128]{1,0:T(8,128)S(1)}, f32[136,128]{1,0:T(8,128)S(1)}, u32[]{:S(2)}, u32[]{:S(2)}) collective-permute-start(f32[136,128]{1,0:T(8,128)S(1)} %get-tuple-element.64), channel_id=1, source_target_pairs={{0,1},{1,2},{2,3},{3,0},{4,5},{5,6},{6,7},{7,4},{8,9},{9,10},{10,1... | collective-permute-start | bytes 208904 | tf_op jit(solution)/shard_map/ppermute | solution.py:394
  82.7 5.5 %collective-permute-start.29 = (f32[136,128]{1,0:T(8,128)S(1)}, f32[136,128]{1,0:T(8,128)S(1)}, u32[]{:S(2)}, u32[]{:S(2)}) collective-permute-start(f32[136,128]{1,0:T(8,128)S(1)} %get-tuple-element.65), channel_id=1, source_target_pairs={{0,2},{1,3},{2,0},{3,1},{4,6},{5,7},{6,4},{7,5},{8,10},{9,11},{10,... | collective-permute-start | bytes 208904 | tf_op jit(solution)/shard_map/ppermute | solution.py:394
  84.2 4.6 %collective-permute-start.30 = (f32[136,128]{1,0:T(8,128)S(1)}, f32[136,128]{1,0:T(8,128)S(1)}, u32[]{:S(2)}, u32[]{:S(2)}) collective-permute-start(f32[136,128]{1,0:T(8,128)S(1)} %get-tuple-element.66), channel_id=1, source_target_pairs={{0,3},{1,0},{2,1},{3,2},{4,7},{5,4},{6,5},{7,6},{8,11},{9,8},{10,9... | collective-permute-start | bytes 208904 | tf_op jit(solution)/shard_map/ppermute | solution.py:394
  (12 other events, 58.7 us)

commit v3 on v2

--- a/solution.py
+++ b/solution.py
@@ -61,6 +61,16 @@
     split = jnp.where(at == 0, a, jnp.where(at == 1, b, jnp.where(at == 2, c, 0.0))).astype(BF16)
     ones = jnp.ones((16, LANES), BF16)
     out_ref[...] = lax.dot_general(split, ones, (((0,), (0,)), ((), ())), preferred_element_type=F32)
+
+
+def diagonals():
+    lane = lax.broadcasted_iota(jnp.int32, (8, LANES), 1)
+    row = lax.broadcasted_iota(jnp.int32, (8, LANES), 0)
+    return [lane == row + 8 * s for s in range(LANES // 8)]
+
+
+def fold(part):
+    return jnp.sum(part, axis=0, keepdims=True)
 
 
 def eight(k):
@@ -157,7 +167,7 @@
 def first_kernel(peers, xplan, yplan, me_ref, pot_ref, *refs):
     xcount, ycount = len(xplan), len(yplan)
     xparts, yparts, refs = refs[:xcount], refs[xcount : xcount + ycount], refs[xcount + ycount :]
-    s_ref, l_ref, xn_ref, yn_ref, yo_ref, xs, xw, yw, top_ref, sum_ref = refs
+    s_ref, l_ref, xn_ref, yn_ref, yo_ref, xs, xw, yw = refs
     me_src, me_tgt = me_ref[0] // peers, lax.rem(me_ref[0], peers)
     for part, d in zip(xparts, xplan):
         if d is None:
@@ -193,43 +203,49 @@
                 xw[:, rows], yw[...], (((0,), (0,)), ((), ())), preferred_element_type=F32
             )
         if b > 0:
-            for r in range((b - 1) * step, b * step, 8):
-                rows = pl.ds(r, 8)
-                lanes_log_sum([s_ref[rows, chunk(c)] for c in range(width // LANES)], rows, pot8, top_ref, sum_ref)
-    l_ref[0] = join_lanes(top_ref, sum_ref)
+            for r in range((b - 1) * step, b * step, LANES):
+                tops = sums = jnp.zeros((8, LANES), F32)
+                for i, own in enumerate(diagonals()):
+                    rows = pl.ds(r + 8 * i, 8)
+                    z = [s_ref[rows, chunk(c)] + pot8[:, c * LANES : (c + 1) * LANES] for c in range(width // LANES)]
+                    part = tree(jnp.maximum, z)
+                    total = tree(jnp.add, [jnp.exp2(v - part) for v in z])
+                    top = jnp.max(part, axis=1, keepdims=True)
+                    tops = jnp.where(own, top, tops)
+                    sums = jnp.where(own, jnp.sum(total * jnp.exp2(part - top), axis=1, keepdims=True), sums)
+                l_ref[0, :, pl.ds(r, LANES)] = fold(tops) + jnp.log2(fold(sums))
 
 
 def src_first_kernel(count, s_ref, mass_ref, *refs):
     parts, (f_ref, p_ref, top_ref, l_ref, wide) = refs[:count], refs[count:]
     f = mass_ref[...] - whole_log_sum(parts)
     f_ref[...] = f
-    across(f, wide)
     n, width = s_ref.shape
     cols = width // LANES
-
-    def load(k):
-        rows = eight(k)
-        f = wide[rows, :]
-        return [s_ref[rows, chunk(c)] + f for c in range(cols)]
-
-    def find(k, top):
-        return tuple(jnp.maximum(t, v) for t, v in zip(top, load(k)))
-
-    tops = lax.fori_loop(1, n // 8, find, tuple(load(0)), unroll=4)
+    f8 = jnp.broadcast_to(f, (8, n))
+    tops = [None] * cols
+    for block in range(0, n, LANES):
+        for i, own in enumerate(diagonals()):
+            rows = pl.ds(block + 8 * i, 8)
+            here = jnp.sum(jnp.where(own, f8[:, block : block + LANES], 0.0), axis=1, keepdims=True)
+            wide[rows, :] = jnp.broadcast_to(here, (8, LANES))
+            z = [s_ref[rows, chunk(c)] + here for c in range(cols)]
+            tops = [v if t is None else jnp.maximum(t, v) for t, v in zip(tops, z)]
     top = jnp.concatenate([jnp.max(t, axis=0, keepdims=True) for t in tops], axis=1)
     top8 = jnp.broadcast_to(top, (8, width))
 
     def add(k, total):
         rows = eight(k)
+        here = wide[rows, :]
         out = []
-        for c, (a, v) in enumerate(zip(total, load(k))):
-            e = jnp.exp2(v - top8[:, c * LANES : (c + 1) * LANES])
+        for c, a in enumerate(total):
+            e = jnp.exp2((s_ref[rows, chunk(c)] + here) - top8[:, c * LANES : (c + 1) * LANES])
             p_ref[rows, chunk(c)] = e
             out.append(a + e)
         return tuple(out)
 
     zero = tuple(jnp.zeros((8, LANES), F32) for _ in range(cols))
-    sums = lax.fori_loop(0, n // 8, add, zero, unroll=4)
+    sums = lax.fori_loop(0, n // 8, add, zero, unroll=16)
     total = jnp.concatenate([jnp.sum(a, axis=0, keepdims=True) for a in sums], axis=1)
     top_ref[...] = top
     repeat(top + jnp.log2(total), l_ref)
@@ -243,16 +259,15 @@
     for u_ref in u_refs:
         u_ref[...] = change
     u = jnp.exp2(change)
-    across(u, wide)
-
-    def add(k, total):
-        rows = eight(k)
-        f = wide[rows, :]
-        return tuple(a + p_ref[rows, chunk(c)] * f for c, a in enumerate(total))
-
-    zero = tuple(jnp.zeros((8, LANES), F32) for _ in range(cols))
-    parts = lax.fori_loop(0, n // 8, add, zero, unroll=4)
-    total = jnp.concatenate([jnp.sum(a, axis=0, keepdims=True) for a in parts], axis=1)
+    u8 = jnp.broadcast_to(u, (8, n))
+    sums = [None] * cols
+    for block in range(0, n, LANES):
+        for i, own in enumerate(diagonals()):
+            rows = pl.ds(block + 8 * i, 8)
+            here = jnp.sum(jnp.where(own, u8[:, block : block + LANES], 0.0), axis=1, keepdims=True)
+            z = [p_ref[rows, chunk(c)] * here for c in range(cols)]
+            sums = [v if a is None else a + v for a, v in zip(sums, z)]
+    total = jnp.concatenate([jnp.sum(a, axis=0, keepdims=True) for a in sums], axis=1)
     repeat(jnp.log2(total) + w_ref[...], l_ref)
     fine = jnp.logical_and(jnp.min(total) >= LOW, jnp.max(u) <= HIGH)
 
@@ -279,16 +294,15 @@
     n, width = p_ref.shape
     v = jnp.exp2(w)
     v8 = jnp.broadcast_to(v, (8, width))
-
-    def strip(k, _):
-        rows = eight(k)
-        sum_ref[rows, :] = tree(
-            jnp.add, [p_ref[rows, chunk(c)] * v8[:, c * LANES : (c + 1) * LANES] for c in range(width // LANES)]
-        )
-        return 0
-
-    lax.fori_loop(0, n // 8, strip, 0, unroll=4)
-    total = to_row(sum_ref[...])
+    out = []
+    for block in range(0, n, LANES):
+        sums = jnp.zeros((8, LANES), F32)
+        for i, own in enumerate(diagonals()):
+            rows = pl.ds(block + 8 * i, 8)
+            z = [p_ref[rows, chunk(c)] * v8[:, c * LANES : (c + 1) * LANES] for c in range(width // LANES)]
+            sums = jnp.where(own, jnp.sum(tree(jnp.add, z), axis=1, keepdims=True), sums)
+        out.append(fold(sums))
+    total = jnp.concatenate(out, axis=1)
     l_ref[0] = jnp.log2(total)
     fine = jnp.logical_and(jnp.min(total) >= LOW, jnp.max(v) <= HIGH)
 
@@ -454,8 +468,6 @@
             pltpu.VMEM((k, n), F32),
             pltpu.VMEM((4 * k, n), BF16),
             pltpu.VMEM((4 * k, width), BF16),
-            lane,
-            lane,
         ],
         [(SMEM, me)] + put(pot, *xs, *ys),
         cost=pl.CostEstimate(flops=8 * k * n * width, transcendentals=n * width, bytes_accessed=8 * n * width),

time: 89.7 us -> 86.1 us (0.960)
  Pallas kernels: 20.8 us -> 17.2 us
    pallas_call x14, Pallas kernels: 20.8 us -> 17.2 us  [call(): pl.pallas_call(kernel, out_shape=[o if isinstance(o, jax.ShapeDtypeStruct...]
where the time goes in v3:
time: 86.1 us; the launch traced here: 85.8 us
  starting transfers between devices  34.8 us (40%)
  waiting for transfers between devices  30 us (35%)
  Pallas kernels  17.2 us (20%)
  local copies, waits for them, and re-layouts  3.06 us (4%)
    ppermute x24, starting transfers between devices, turn(): return lax.ppermute(v, axis, [(i, (i + d) % size) for i in range(size)])  30.2 us
    ppermute x24, waiting for transfers between devices, turn(): return lax.ppermute(v, axis, [(i, (i + d) % size) for i in range(size)])  25 us
    pallas_call x14, Pallas kernels, call(): pl.pallas_call(kernel, out_shape=[o if isinstance(o, jax.ShapeDtypeStruct...  17.2 us
    ppermute x7, waiting for transfers between devices, flip(): return lax.ppermute(v, axis, [(i, i ^ bit) for i in range(size)])  5.02 us
    ppermute x7, starting transfers between devices, flip(): return lax.ppermute(v, axis, [(i, i ^ bit) for i in range(size)])  4.6 us
    unnamed x10, local copies, waits for them, and re-layouts  3.06 us
  transfers between devices with their start and end apart: 31, of which 24 were waited for; matrix products, arithmetic and copies ran while one was open for 0% of the time, Pallas kernels for 0%

profile of v3, /device:TPU:0, one launch (start us, length us, event | category | flops | bytes accessed | tf_op | source)
XLA Modules:
  0.0 85.8 jit_solution(4612468986323312286)
XLA Ops:
  0.6 3.9 %collective-permute-start = (f32[16,1024]{1,0:T(8,128)}, f32[16,1024]{1,0:T(8,128)S(1)}, u32[]{:S(2)}, u32[]{:S(2)}) collective-permute-start(f32[16,1024]{1,0:T(8,128)} %refs_1_.1), channel_id=1, source_target_pairs={{0,3},{1,0},{2,1},{3,2},{4,7},{5,4},{6,5},{7,6},{8,11},{9,8},{10,9... | collective-permute-start | bytes 196616 | tf_op jit(solution)/shard_map/ppermute | solution.py:408
  4.6 3.6 %collective-permute-start.3 = (f32[8,2048]{1,0:T(8,128)}, f32[8,2048]{1,0:T(8,128)S(1)}, u32[]{:S(2)}, u32[]{:S(2)}) collective-permute-start(f32[8,2048]{1,0:T(8,128)} %refs_2_.1), channel_id=1, source_target_pairs={{0,24},{4,28},{8,16},{12,20},{16,8},{20,12},{24,0},{28,4},{1,25},{... | collective-permute-start | bytes 196616 | tf_op jit(solution)/shard_map/ppermute | solution.py:412
  9.7 2.4 %collective-permute-start.4 = (f32[16,1024]{1,0:T(8,128)}, f32[16,1024]{1,0:T(8,128)S(1)}, u32[]{:S(2)}, u32[]{:S(2)}) collective-permute-start(f32[16,1024]{1,0:T(8,128)} %refs_1_.1), channel_id=1, source_target_pairs={{0,1},{1,2},{2,3},{3,0},{4,5},{5,6},{6,7},{7,4},{8,9},{9,10},{10,1... | collective-permute-start | bytes 196616 | tf_op jit(solution)/shard_map/ppermute | solution.py:408
  15.1 1.5 %collective-permute-done.6.refs_5_ = f32[32,2048]{1,0:T(8,128)S(1)} collective-permute-done((f32[32,2048]{1,0:T(8,128)S(1)}, f32[32,2048]{1,0:T(8,128)S(1)}, u32[]{:S(2)}, u32[]{:S(2)}) %collective-permute-start.6) | collective-permute-done | bytes 262176 | tf_op jit(solution)/shard_map/ppermute | solution.py:412
  16.6 2.6 %shard_map.78 = (f32[1024,2048]{1,0:T(8,128)S(1)}, f32[1,1,1024]{2,1,0:T(1,128)S(1)}, f32[1,1024]{1,0:T(1,128)S(1)}, f32[1,2048]{1,0:T(1,128)S(1)}, f32[64,2048]{1,0:T(8,128)S(1)}) custom-call(s32[1]{0:T(128)} %bitcast.me_ref, f32[1,2048]{1,0:T(1,128)S(1)} %get-tuple-element.35.pot_ref, f32[16,1024]{1,0:T(8,128)S(1)} %get-tuple-element.40.refs_0_, ...), custom_call_target="tpu_custom_call" | custom-call | flops 1073741824 | bytes 16777216 | tf_op jit(solution)/shard_map/pallas_call | solution.py:392
  19.3 1.5 %collective-permute-start.9 = (f32[1,1,1024]{2,1,0:T(1,128)S(1)}, f32[1,1,1024]{2,1,0:T(1,128)S(1)}, u32[]{:S(2)}, u32[]{:S(2)}) collective-permute-start(f32[1,1,1024]{2,1,0:T(1,128)S(1)} %get-tuple-element.48.refs_0_), channel_id=1, source_target_pairs={{0,3},{1,0},{2,1},{3,2},{4,7},{5,4},{6,5},{7,6},{8,11},{9,8},{10,9... | collective-permute-start | bytes 12296 | tf_op jit(solution)/shard_map/ppermute | solution.py:408
  20.8 1.5 %collective-permute-start.8 = (f32[1,1,1024]{2,1,0:T(1,128)S(1)}, f32[1,1,1024]{2,1,0:T(1,128)S(1)}, u32[]{:S(2)}, u32[]{:S(2)}) collective-permute-start(f32[1,1,1024]{2,1,0:T(1,128)S(1)} %get-tuple-element.48.refs_0_), channel_id=1, source_target_pairs={{0,2},{1,3},{2,0},{3,1},{4,6},{5,7},{6,4},{7,5},{8,10},{9,11},{10,... | collective-permute-start | bytes 12296 | tf_op jit(solution)/shard_map/ppermute | solution.py:408
  24.4 2.4 %collective-permute-done.7.refs_1_ = f32[1,1,1024]{2,1,0:T(1,128)S(1)} collective-permute-done((f32[1,1,1024]{2,1,0:T(1,128)S(1)}, f32[1,1,1024]{2,1,0:T(1,128)S(1)}, u32[]{:S(2)}, u32[]{:S(2)}) %collective-permute-start.7) | collective-permute-done | bytes 4128 | tf_op jit(solution)/shard_map/ppermute | solution.py:408
  26.8 2.4 %shard_map.80 = (f32[1,1024]{1,0:T(1,128)S(1)}, f32[1024,2048]{1,0:T(8,128)S(1)}, f32[1,2048]{1,0:T(1,128)S(1)}, f32[1,1,2048]{2,1,0:T(1,128)S(1)}) custom-call(f32[1024,2048]{1,0:T(8,128)S(1)} %get-tuple-element.45.s_ref, f32[1,1024]{1,0:T(1,128)S(1)} %shard_map.79.mass_ref, f32[1,1,1024]{2,1,0:T(1,128)S(1)} %get-tuple-element.48.refs_0_, ...), custom_call_target="tpu_custom_call" | custom-call | tf_op jit(solution)/shard_map/pallas_call | solution.py:392
  29.2 2.5 %collective-permute-start.12 = (f32[1,1,2048]{2,1,0:T(1,128)S(1)}, f32[1,1,2048]{2,1,0:T(1,128)S(1)}, u32[]{:S(2)}, u32[]{:S(2)}) collective-permute-start(f32[1,1,2048]{2,1,0:T(1,128)S(1)} %get-tuple-element.52.refs_0_), channel_id=1, source_target_pairs={{0,24},{4,28},{8,0},{12,4},{16,8},{20,12},{24,16},{28,20},{1,25},{... | collective-permute-start | bytes 24584 | tf_op jit(solution)/shard_map/ppermute | solution.py:408
  31.9 1.9 %collective-permute-start.10 = (f32[1,1,2048]{2,1,0:T(1,128)S(1)}, f32[1,1,2048]{2,1,0:T(1,128)S(1)}, u32[]{:S(2)}, u32[]{:S(2)}) collective-permute-start(f32[1,1,2048]{2,1,0:T(1,128)S(1)} %get-tuple-element.52.refs_0_), channel_id=1, source_target_pairs={{0,8},{4,12},{8,16},{12,20},{16,24},{20,28},{24,0},{28,4},{1,9},{5... | collective-permute-start | bytes 24584 | tf_op jit(solution)/shard_map/ppermute | solution.py:408
  33.9 2.4 %collective-permute-done.11.refs_2_ = f32[1,1,2048]{2,1,0:T(1,128)S(1)} collective-permute-done((f32[1,1,2048]{2,1,0:T(1,128)S(1)}, f32[1,1,2048]{2,1,0:T(1,128)S(1)}, u32[]{:S(2)}, u32[]{:S(2)}) %collective-permute-start.11) | collective-permute-done | bytes 8224 | tf_op jit(solution)/shard_map/ppermute | solution.py:408
  39.8 1.5 %collective-permute-start.15 = (f32[1,1,1024]{2,1,0:T(1,128)S(1)}, f32[1,1,1024]{2,1,0:T(1,128)S(1)}, u32[]{:S(2)}, u32[]{:S(2)}) collective-permute-start(f32[1,1,1024]{2,1,0:T(1,128)S(1)} %get-tuple-element.55.refs_0_), channel_id=1, source_target_pairs={{0,2},{1,3},{2,0},{3,1},{4,6},{5,7},{6,4},{7,5},{8,10},{9,11},{10,... | collective-permute-start | bytes 12296 | tf_op jit(solution)/shard_map/ppermute | solution.py:408
  43.4 2.4 %collective-permute-done.14.refs_1_ = f32[1,1,1024]{2,1,0:T(1,128)S(1)} collective-permute-done((f32[1,1,1024]{2,1,0:T(1,128)S(1)}, f32[1,1,1024]{2,1,0:T(1,128)S(1)}, u32[]{:S(2)}, u32[]{:S(2)}) %collective-permute-start.14) | collective-permute-done | bytes 4128 | tf_op jit(solution)/shard_map/ppermute | solution.py:408
  47.9 1.9 %collective-permute-start.17 = (f32[1,1,2048]{2,1,0:T(1,128)S(1)}, f32[1,1,2048]{2,1,0:T(1,128)S(1)}, u32[]{:S(2)}, u32[]{:S(2)}) collective-permute-start(f32[1,1,2048]{2,1,0:T(1,128)S(1)} %shard_map.83.refs_0_), channel_id=1, source_target_pairs={{0,8},{4,12},{8,16},{12,20},{16,24},{20,28},{24,0},{28,4},{1,9},{5... | collective-permute-start | bytes 24584 | tf_op jit(solution)/shard_map/ppermute | solution.py:408
  50.3 1.5 %collective-permute-done.18.refs_2_ = f32[1,1,2048]{2,1,0:T(1,128)S(1)} collective-permute-done((f32[1,1,2048]{2,1,0:T(1,128)S(1)}, f32[1,1,2048]{2,1,0:T(1,128)S(1)}, u32[]{:S(2)}, u32[]{:S(2)}) %collective-permute-start.18) | collective-permute-done | bytes 8224 | tf_op jit(solution)/shard_map/ppermute | solution.py:408
  51.8 1.5 %collective-permute-done.17.refs_1_ = f32[1,1,2048]{2,1,0:T(1,128)S(1)} collective-permute-done((f32[1,1,2048]{2,1,0:T(1,128)S(1)}, f32[1,1,2048]{2,1,0:T(1,128)S(1)}, u32[]{:S(2)}, u32[]{:S(2)}) %collective-permute-start.17) | collective-permute-done | bytes 8224 | tf_op jit(solution)/shard_map/ppermute | solution.py:408
  60.1 1.4 %collective-permute-done.21.refs_1_ = f32[1,1,1024]{2,1,0:T(1,128)S(1)} collective-permute-done((f32[1,1,1024]{2,1,0:T(1,128)S(1)}, f32[1,1,1024]{2,1,0:T(1,128)S(1)}, u32[]{:S(2)}, u32[]{:S(2)}) %collective-permute-start.21) | collective-permute-done | bytes 4128 | tf_op jit(solution)/shard_map/ppermute | solution.py:408
  61.5 3.4 %shard_map.86 = (f32[1,1024]{1,0:T(1,128)S(1)}, f32[1,1,2048]{2,1,0:T(1,128)S(1)}) custom-call(f32[1024,2048]{1,0:T(8,128)S(1)} %get-tuple-element.45.s_ref, f32[1024,2048]{1,0:T(8,128)S(1)} %get-tuple-element.49.p_ref, f32[1,1024]{1,0:T(1,128)S(1)} %shard_map.79.mass_ref, f32[1,1024]{1,0:T(1,128)S(1)} %get-tuple-element.50.f_ref, ...), custom_call_target="tpu_custom_call" | custom-call | tf_op jit(solution)/shard_map/pallas_call | solution.py:392
  67.0 1.7 %collective-permute-done.26.refs_3_ = f32[1,1,2048]{2,1,0:T(1,128)S(1)} collective-permute-done((f32[1,1,2048]{2,1,0:T(1,128)S(1)}, f32[1,1,2048]{2,1,0:T(1,128)S(1)}, u32[]{:S(2)}, u32[]{:S(2)}) %collective-permute-start.26) | collective-permute-done | bytes 8224 | tf_op jit(solution)/shard_map/ppermute | solution.py:408
  68.7 1.8 %collective-permute-done.25.refs_2_ = f32[1,1,2048]{2,1,0:T(1,128)S(1)} collective-permute-done((f32[1,1,2048]{2,1,0:T(1,128)S(1)}, f32[1,1,2048]{2,1,0:T(1,128)S(1)}, u32[]{:S(2)}, u32[]{:S(2)}) %collective-permute-start.25) | collective-permute-done | bytes 8224 | tf_op jit(solution)/shard_map/ppermute | solution.py:408
  72.7 5.7 %shard_map.88 = (f32[1,1024]{1,0:T(1,128)}, f32[1,2048]{1,0:T(1,128)}, f32[136,128]{1,0:T(8,128)S(1)}, f32[136,128]{1,0:T(8,128)S(1)}, f32[136,128]{1,0:T(8,128)S(1)}, /*index=5*/f32[136,128]{1,0:T(8,128)S(1)}) custom-call(s32[1]{0:T(128)} %bitcast.me_ref, f32[1024,2048]{1,0:T(8,128)S(1)} %get-tuple-element.45.s_ref, ...), custom_call_target="tpu_custom_call" | custom-call | tf_op jit(solution)/shard_map/pallas_call | solution.py:392
  79.1 1.5 %collective-permute-start.29 = (f32[136,128]{1,0:T(8,128)S(1)}, f32[136,128]{1,0:T(8,128)S(1)}, u32[]{:S(2)}, u32[]{:S(2)}) collective-permute-start(f32[136,128]{1,0:T(8,128)S(1)} %get-tuple-element.65), channel_id=1, source_target_pairs={{0,2},{1,3},{2,0},{3,1},{4,6},{5,7},{6,4},{7,5},{8,10},{9,11},{10,... | collective-permute-start | bytes 208904 | tf_op jit(solution)/shard_map/ppermute | solution.py:408
  80.6 2.3 %collective-permute-start.30 = (f32[136,128]{1,0:T(8,128)S(1)}, f32[136,128]{1,0:T(8,128)S(1)}, u32[]{:S(2)}, u32[]{:S(2)}) collective-permute-start(f32[136,128]{1,0:T(8,128)S(1)} %get-tuple-element.66), channel_id=1, source_target_pairs={{0,3},{1,0},{2,1},{3,2},{4,7},{5,4},{6,5},{7,6},{8,11},{9,8},{10,9... | collective-permute-start | bytes 208904 | tf_op jit(solution)/shard_map/ppermute | solution.py:408
  (62 shorter events, 29.5 us)
Async XLA Ops:
  0.6 7.6 %collective-permute-start = (f32[16,1024]{1,0:T(8,128)}, f32[16,1024]{1,0:T(8,128)S(1)}, u32[]{:S(2)}, u32[]{:S(2)}) collective-permute-start(f32[16,1024]{1,0:T(8,128)} %refs_1_.1), channel_id=1, source_target_pairs={{0,3},{1,0},{2,1},{3,2},{4,7},{5,4},{6,5},{7,6},{8,11},{9,8},{10,9... | collective-permute-start | bytes 196616 | tf_op jit(solution)/shard_map/ppermute | solution.py:408
  4.6 9.9 %collective-permute-start.3 = (f32[8,2048]{1,0:T(8,128)}, f32[8,2048]{1,0:T(8,128)S(1)}, u32[]{:S(2)}, u32[]{:S(2)}) collective-permute-start(f32[8,2048]{1,0:T(8,128)} %refs_2_.1), channel_id=1, source_target_pairs={{0,24},{4,28},{8,16},{12,20},{16,8},{20,12},{24,0},{28,4},{1,25},{... | collective-permute-start | bytes 196616 | tf_op jit(solution)/shard_map/ppermute | solution.py:412
  8.2 6.3 %collective-permute-start.2 = (f32[8,2048]{1,0:T(8,128)}, f32[8,2048]{1,0:T(8,128)S(1)}, u32[]{:S(2)}, u32[]{:S(2)}) collective-permute-start(f32[8,2048]{1,0:T(8,128)} %refs_2_.1), channel_id=1, source_target_pairs={{0,16},{4,20},{8,24},{12,28},{16,0},{20,4},{24,8},{28,12},{1,17},{... | collective-permute-start | bytes 196616 | tf_op jit(solution)/shard_map/ppermute | solution.py:412
  8.2 6.3 %collective-permute-start.1 = (f32[8,2048]{1,0:T(8,128)}, f32[8,2048]{1,0:T(8,128)S(1)}, u32[]{:S(2)}, u32[]{:S(2)}) collective-permute-start(f32[8,2048]{1,0:T(8,128)} %refs_2_.1), channel_id=1, source_target_pairs={{0,8},{4,12},{8,0},{12,4},{16,24},{20,28},{24,16},{28,20},{1,9},{5... | collective-permute-start | bytes 196616 | tf_op jit(solution)/shard_map/ppermute | solution.py:412
  9.0 5.6 %collective-permute-start.5 = (f32[16,1024]{1,0:T(8,128)}, f32[16,1024]{1,0:T(8,128)S(1)}, u32[]{:S(2)}, u32[]{:S(2)}) collective-permute-start(f32[16,1024]{1,0:T(8,128)} %refs_1_.1), channel_id=1, source_target_pairs={{0,2},{1,3},{2,0},{3,1},{4,6},{5,7},{6,4},{7,5},{8,10},{9,11},{10,... | collective-permute-start | bytes 196616 | tf_op jit(solution)/shard_map/ppermute | solution.py:408
  9.7 5.4 %collective-permute-start.4 = (f32[16,1024]{1,0:T(8,128)}, f32[16,1024]{1,0:T(8,128)S(1)}, u32[]{:S(2)}, u32[]{:S(2)}) collective-permute-start(f32[16,1024]{1,0:T(8,128)} %refs_1_.1), channel_id=1, source_target_pairs={{0,1},{1,2},{2,3},{3,0},{4,5},{5,6},{6,7},{7,4},{8,9},{9,10},{10,1... | collective-permute-start | bytes 196616 | tf_op jit(solution)/shard_map/ppermute | solution.py:408
  19.3 4.1 %collective-permute-start.9 = (f32[1,1,1024]{2,1,0:T(1,128)S(1)}, f32[1,1,1024]{2,1,0:T(1,128)S(1)}, u32[]{:S(2)}, u32[]{:S(2)}) collective-permute-start(f32[1,1,1024]{2,1,0:T(1,128)S(1)} %get-tuple-element.48.refs_0_), channel_id=1, source_target_pairs={{0,3},{1,0},{2,1},{3,2},{4,7},{5,4},{6,5},{7,6},{8,11},{9,8},{10,9... | collective-permute-start | bytes 12296 | tf_op jit(solution)/shard_map/ppermute | solution.py:408
  22.3 4.5 %collective-permute-start.7 = (f32[1,1,1024]{2,1,0:T(1,128)S(1)}, f32[1,1,1024]{2,1,0:T(1,128)S(1)}, u32[]{:S(2)}, u32[]{:S(2)}) collective-permute-start(f32[1,1,1024]{2,1,0:T(1,128)S(1)} %get-tuple-element.48.refs_0_), channel_id=1, source_target_pairs={{0,1},{1,2},{2,3},{3,0},{4,5},{5,6},{6,7},{7,4},{8,9},{9,10},{10,1... | collective-permute-start | bytes 12296 | tf_op jit(solution)/shard_map/ppermute | solution.py:408
  29.2 4.7 %collective-permute-start.12 = (f32[1,1,2048]{2,1,0:T(1,128)S(1)}, f32[1,1,2048]{2,1,0:T(1,128)S(1)}, u32[]{:S(2)}, u32[]{:S(2)}) collective-permute-start(f32[1,1,2048]{2,1,0:T(1,128)S(1)} %get-tuple-element.52.refs_0_), channel_id=1, source_target_pairs={{0,24},{4,28},{8,0},{12,4},{16,8},{20,12},{24,16},{28,20},{1,25},{... | collective-permute-start | bytes 24584 | tf_op jit(solution)/shard_map/ppermute | solution.py:408
  31.7 4.5 %collective-permute-start.11 = (f32[1,1,2048]{2,1,0:T(1,128)S(1)}, f32[1,1,2048]{2,1,0:T(1,128)S(1)}, u32[]{:S(2)}, u32[]{:S(2)}) collective-permute-start(f32[1,1,2048]{2,1,0:T(1,128)S(1)} %get-tuple-element.52.refs_0_), channel_id=1, source_target_pairs={{0,16},{4,20},{8,24},{12,28},{16,0},{20,4},{24,8},{28,12},{1,17},{... | collective-permute-start | bytes 24584 | tf_op jit(solution)/shard_map/ppermute | solution.py:408
  31.9 5.4 %collective-permute-start.10 = (f32[1,1,2048]{2,1,0:T(1,128)S(1)}, f32[1,1,2048]{2,1,0:T(1,128)S(1)}, u32[]{:S(2)}, u32[]{:S(2)}) collective-permute-start(f32[1,1,2048]{2,1,0:T(1,128)S(1)} %get-tuple-element.52.refs_0_), channel_id=1, source_target_pairs={{0,8},{4,12},{8,16},{12,20},{16,24},{20,28},{24,0},{28,4},{1,9},{5... | collective-permute-start | bytes 24584 | tf_op jit(solution)/shard_map/ppermute | solution.py:408
  39.4 3.7 %collective-permute-start.16 = (f32[1,1,1024]{2,1,0:T(1,128)S(1)}, f32[1,1,1024]{2,1,0:T(1,128)S(1)}, u32[]{:S(2)}, u32[]{:S(2)}) collective-permute-start(f32[1,1,1024]{2,1,0:T(1,128)S(1)} %get-tuple-element.55.refs_0_), channel_id=1, source_target_pairs={{0,3},{1,0},{2,1},{3,2},{4,7},{5,4},{6,5},{7,6},{8,11},{9,8},{10,9... | collective-permute-start | bytes 12296 | tf_op jit(solution)/shard_map/ppermute | solution.py:408
  41.3 4.5 %collective-permute-start.14 = (f32[1,1,1024]{2,1,0:T(1,128)S(1)}, f32[1,1,1024]{2,1,0:T(1,128)S(1)}, u32[]{:S(2)}, u32[]{:S(2)}) collective-permute-start(f32[1,1,1024]{2,1,0:T(1,128)S(1)} %get-tuple-element.55.refs_0_), channel_id=1, source_target_pairs={{0,1},{1,2},{2,3},{3,0},{4,5},{5,6},{6,7},{7,4},{8,9},{9,10},{10,1... | collective-permute-start | bytes 12296 | tf_op jit(solution)/shard_map/ppermute | solution.py:408
  46.6 3.7 %collective-permute-start.19 = (f32[1,1,2048]{2,1,0:T(1,128)S(1)}, f32[1,1,2048]{2,1,0:T(1,128)S(1)}, u32[]{:S(2)}, u32[]{:S(2)}) collective-permute-start(f32[1,1,2048]{2,1,0:T(1,128)S(1)} %shard_map.83.refs_0_), channel_id=1, source_target_pairs={{0,24},{4,28},{8,0},{12,4},{16,8},{20,12},{24,16},{28,20},{1,25},{... | collective-permute-start | bytes 24584 | tf_op jit(solution)/shard_map/ppermute | solution.py:408
  47.2 4.5 %collective-permute-start.18 = (f32[1,1,2048]{2,1,0:T(1,128)S(1)}, f32[1,1,2048]{2,1,0:T(1,128)S(1)}, u32[]{:S(2)}, u32[]{:S(2)}) collective-permute-start(f32[1,1,2048]{2,1,0:T(1,128)S(1)} %shard_map.83.refs_0_), channel_id=1, source_target_pairs={{0,16},{4,20},{8,24},{12,28},{16,0},{20,4},{24,8},{28,12},{1,17},{... | collective-permute-start | bytes 24584 | tf_op jit(solution)/shard_map/ppermute | solution.py:408
  47.9 5.4 %collective-permute-start.17 = (f32[1,1,2048]{2,1,0:T(1,128)S(1)}, f32[1,1,2048]{2,1,0:T(1,128)S(1)}, u32[]{:S(2)}, u32[]{:S(2)}) collective-permute-start(f32[1,1,2048]{2,1,0:T(1,128)S(1)} %shard_map.83.refs_0_), channel_id=1, source_target_pairs={{0,8},{4,12},{8,16},{12,20},{16,24},{20,28},{24,0},{28,4},{1,9},{5... | collective-permute-start | bytes 24584 | tf_op jit(solution)/shard_map/ppermute | solution.py:408
  55.4 3.7 %collective-permute-start.23 = (f32[1,1,1024]{2,1,0:T(1,128)S(1)}, f32[1,1,1024]{2,1,0:T(1,128)S(1)}, u32[]{:S(2)}, u32[]{:S(2)}) collective-permute-start(f32[1,1,1024]{2,1,0:T(1,128)S(1)} %shard_map.85.refs_0_), channel_id=1, source_target_pairs={{0,3},{1,0},{2,1},{3,2},{4,7},{5,4},{6,5},{7,6},{8,11},{9,8},{10,9... | collective-permute-start | bytes 12296 | tf_op jit(solution)/shard_map/ppermute | solution.py:408
  57.0 4.5 %collective-permute-start.21 = (f32[1,1,1024]{2,1,0:T(1,128)S(1)}, f32[1,1,1024]{2,1,0:T(1,128)S(1)}, u32[]{:S(2)}, u32[]{:S(2)}) collective-permute-start(f32[1,1,1024]{2,1,0:T(1,128)S(1)} %shard_map.85.refs_0_), channel_id=1, source_target_pairs={{0,1},{1,2},{2,3},{3,0},{4,5},{5,6},{6,7},{7,4},{8,9},{9,10},{10,1... | collective-permute-start | bytes 12296 | tf_op jit(solution)/shard_map/ppermute | solution.py:408
  65.0 3.8 %collective-permute-start.26 = (f32[1,1,2048]{2,1,0:T(1,128)S(1)}, f32[1,1,2048]{2,1,0:T(1,128)S(1)}, u32[]{:S(2)}, u32[]{:S(2)}) collective-permute-start(f32[1,1,2048]{2,1,0:T(1,128)S(1)} %get-tuple-element.60.refs_0_), channel_id=1, source_target_pairs={{0,24},{4,28},{8,0},{12,4},{16,8},{20,12},{24,16},{28,20},{1,25},{... | collective-permute-start | bytes 24584 | tf_op jit(solution)/shard_map/ppermute | solution.py:408
  66.0 4.5 %collective-permute-start.25 = (f32[1,1,2048]{2,1,0:T(1,128)S(1)}, f32[1,1,2048]{2,1,0:T(1,128)S(1)}, u32[]{:S(2)}, u32[]{:S(2)}) collective-permute-start(f32[1,1,2048]{2,1,0:T(1,128)S(1)} %get-tuple-element.60.refs_0_), channel_id=1, source_target_pairs={{0,16},{4,20},{8,24},{12,28},{16,0},{20,4},{24,8},{28,12},{1,17},{... | collective-permute-start | bytes 24584 | tf_op jit(solution)/shard_map/ppermute | solution.py:408
  66.0 5.4 %collective-permute-start.24 = (f32[1,1,2048]{2,1,0:T(1,128)S(1)}, f32[1,1,2048]{2,1,0:T(1,128)S(1)}, u32[]{:S(2)}, u32[]{:S(2)}) collective-permute-start(f32[1,1,2048]{2,1,0:T(1,128)S(1)} %get-tuple-element.60.refs_0_), channel_id=1, source_target_pairs={{0,8},{4,12},{8,16},{12,20},{16,24},{20,28},{24,0},{28,4},{1,9},{5... | collective-permute-start | bytes 24584 | tf_op jit(solution)/shard_map/ppermute | solution.py:408
  78.4 5.6 %collective-permute-start.28 = (f32[136,128]{1,0:T(8,128)S(1)}, f32[136,128]{1,0:T(8,128)S(1)}, u32[]{:S(2)}, u32[]{:S(2)}) collective-permute-start(f32[136,128]{1,0:T(8,128)S(1)} %get-tuple-element.64), channel_id=1, source_target_pairs={{0,1},{1,2},{2,3},{3,0},{4,5},{5,6},{6,7},{7,4},{8,9},{9,10},{10,1... | collective-permute-start | bytes 208904 | tf_op jit(solution)/shard_map/ppermute | solution.py:408
  79.1 5.5 %collective-permute-start.29 = (f32[136,128]{1,0:T(8,128)S(1)}, f32[136,128]{1,0:T(8,128)S(1)}, u32[]{:S(2)}, u32[]{:S(2)}) collective-permute-start(f32[136,128]{1,0:T(8,128)S(1)} %get-tuple-element.65), channel_id=1, source_target_pairs={{0,2},{1,3},{2,0},{3,1},{4,6},{5,7},{6,4},{7,5},{8,10},{9,11},{10,... | collective-permute-start | bytes 208904 | tf_op jit(solution)/shard_map/ppermute | solution.py:408
  80.6 4.6 %collective-permute-start.30 = (f32[136,128]{1,0:T(8,128)S(1)}, f32[136,128]{1,0:T(8,128)S(1)}, u32[]{:S(2)}, u32[]{:S(2)}) collective-permute-start(f32[136,128]{1,0:T(8,128)S(1)} %get-tuple-element.66), channel_id=1, source_target_pairs={{0,3},{1,0},{2,1},{3,2},{4,7},{5,4},{6,5},{7,6},{8,11},{9,8},{10,9... | collective-permute-start | bytes 208904 | tf_op jit(solution)/shard_map/ppermute | solution.py:408
  (12 other events, 57.1 us)
